TPU v7x, 128 devices: a whole 4x4x4 slice. The times are simulated.
128 devices in a mesh: pr: 4 (over x), pc: 32 (over y, z, core).
Axes of the slice: x: 4, y: 4, z: 4, core: 2. Of those that a mesh axis runs over, the one named last changes fastest.
Arguments:
- matrix: float32 [4, 8, 512, 32, 1, 512], P('pr', None, None, 'pc'), may hold values from -8 to 9, as said below
Outputs:
- factored: float32 [4, 8, 512, 32, 1, 512], P('pr', None, None, 'pc')
Inputs may be any that keep to these rules, and one draw needn't show every extreme that they name: The matrix A that matrix stores is symmetric and positive definite.
All inputs are finite; a program needn't handle non-finite values.
Results may differ from a plain program's by a relative error of at most 0.00012.
Values sent between devices are 32-bit elements; how exact they have to be, the bound alone decides.
A program may use at most 128 MiB of HBM per device.

v0:
```python
import jax
import jax.numpy as jnp
from jax import lax
from jax.sharding import PartitionSpec as P

STEPS = 2


def broadcast(value, axis, source):
    kept = jnp.where(lax.axis_index(axis) == source, value, 0).astype(value.dtype)
    return lax.psum(kept, axis)


def solve_panel(corner, column, row_marks, step, eye):
    factor = jnp.tril(jnp.linalg.cholesky(corner))
    inverse = jax.scipy.linalg.solve_triangular(factor, eye, lower=True)
    solved = lax.dot_general(
        column,
        inverse,
        (((1,), (1,)), ((), ())),
        precision=lax.Precision.HIGHEST,
        preferred_element_type=jnp.float32,
    )
    solved = jnp.where(row_marks[:, None] > step, solved, 0.0)
    return (factor, solved)


def body(matrix):
    prows = lax.axis_size("pr")
    pcols = lax.axis_size("pc")
    lrows = matrix.shape[1]
    block = matrix.shape[2]
    lcols = matrix.shape[4]
    local = matrix.reshape(lrows * block, lcols * block)
    row_here = lax.axis_index("pr")
    col_here = lax.axis_index("pc")
    row_blocks = jnp.arange(lrows, dtype=jnp.int32) * prows + row_here
    col_blocks = jnp.arange(lcols, dtype=jnp.int32) * pcols + col_here
    row_marks = jnp.repeat(row_blocks, block)
    col_marks = jnp.repeat(col_blocks, block)
    eye = jnp.eye(block, dtype=jnp.float32)
    for step in range(STEPS):
        row_local = step // prows
        col_local = step // pcols
        root_row = step % prows
        root_col = step % pcols
        row_lo = row_local * block
        col_lo = col_local * block
        corner = local[row_lo : row_lo + block, col_lo : col_lo + block]
        column = local
        corner = broadcast(corner, "pr", root_row)
        factor, solved = solve_panel(corner, column, row_marks, step, eye)
        panel = broadcast(solved, "pc", root_col)
        target = 0 + col_here
        start = target // prows * block
        piece = lax.dynamic_slice_in_dim(panel, start, block, 0)
        pieces = broadcast(piece, "pr", target % prows)
        update = lax.dot_general(
            panel,
            pieces,
            (((1,), (1,)), ((), ())),
            precision=lax.Precision.HIGHEST,
            preferred_element_type=jnp.float32,
        )
        local = local - update
        owns_column = col_here == root_col
        owns_row = row_here == root_row
        column_now = local
        column_new = jnp.where(row_marks[:, None] > step, panel, column_now)
        corner_now = column_new[row_lo : row_lo + block]
        corner_new = jnp.where(owns_row, factor, corner_now)
        column_new = column_new.at[row_lo : row_lo + block].set(corner_new)
        column_new = jnp.where(owns_column, column_new, column_now)
        local = local.at[:, col_lo : col_lo + block].set(column_new)
        row_now = local[row_lo : row_lo + block, :]
        row_new = jnp.where(col_marks[None, :] > step, pieces.T, row_now)
        row_new = jnp.where(owns_row, row_new, row_now)
        local = local.at[row_lo : row_lo + block, :].set(row_new)
    return local.reshape(matrix.shape)


def solution(mesh):
    placed = (P("pr", None, None, "pc", None, None),)
    return jax.shard_map(
        body,
        mesh=mesh,
        in_specs=placed,
        out_specs=P("pr", None, None, "pc", None, None),
        check_vma=False,
    )
```

profile of v0, /device:TPU:7, one launch (start us, length us, event | category | flops | bytes accessed | tf_op | source)
XLA Modules:
  0.0 862.6 jit_solution(2307349846067483647)
XLA Ops:
  19.0 38.3 %all-reduce.8.cloned.1.call-done = f32[512,512]{0,1:T(8,128)} async-done(((f32[512,512]{0,1:T(8,128)}), f32[512,512]{0,1:T(8,128)}) %all-reduce.8.cloned.1.call-update) | async-done | bytes 1048592 | tf_op jit(solution)/shard_map/psum | solution.py:11
  60.4 11.7 %cholesky.286 = f32[128,128]{1,0:T(8,128)S(1)} custom-call(f32[128,128]{1,0:T(8,128)S(1)} %cholesky.426), custom_call_target="Cholesky" | custom-call | tf_op jit(solution)/shard_map/jit(cholesky)/cholesky | solution.py:15
  72.1 9.8 %custom-call.27 = f32[1,128,128]{1,2,0:T(8,128)S(1)} custom-call(f32[1,128,128]{2,1,0:T(8,128)S(1)} %get-tuple-element.152), custom_call_target="InvertDiagBlocksLowerTriangular" | custom-call | tf_op jit(solution)/shard_map/jit(cholesky)/cholesky | solution.py:15
  82.7 20.4 %cholesky.305 = f32[128,128]{1,0:T(8,128)S(1)} custom-call(f32[128,128]{1,0:T(8,128)S(1)} %cholesky.430), custom_call_target="Cholesky" | custom-call | tf_op jit(solution)/shard_map/jit(cholesky)/cholesky | solution.py:15
  103.2 9.8 %custom-call.28 = f32[1,128,128]{1,2,0:T(8,128)S(1)} custom-call(f32[1,128,128]{2,1,0:T(8,128)S(1)} %get-tuple-element.149), custom_call_target="InvertDiagBlocksLowerTriangular" | custom-call | tf_op jit(solution)/shard_map/jit(cholesky)/cholesky | solution.py:15
  113.7 11.7 %cholesky.326 = f32[128,128]{1,0:T(8,128)S(1)} custom-call(f32[128,128]{1,0:T(8,128)S(1)} %cholesky.435), custom_call_target="Cholesky" | custom-call | tf_op jit(solution)/shard_map/jit(cholesky)/cholesky | solution.py:15
  126.2 9.8 %custom-call.29 = f32[1,128,128]{1,2,0:T(8,128)S(1)} custom-call(f32[1,128,128]{2,1,0:T(8,128)S(1)} %get-tuple-element.146), custom_call_target="InvertDiagBlocksLowerTriangular" | custom-call | tf_op jit(solution)/shard_map/jit(cholesky)/cholesky | solution.py:15
  136.6 11.9 %cholesky.343 = f32[128,128]{1,0:T(8,128)S(1)} custom-call(f32[128,128]{1,0:T(8,128)S(1)} %convolution_subtract_fusion.13), custom_call_target="Cholesky" | custom-call | tf_op jit(solution)/shard_map/jit(cholesky)/cholesky | solution.py:15
  152.5 8.1 while.12
  161.4 40.1 %custom-call.30 = f32[4,128,128]{1,2,0:T(8,128)S(1)} custom-call(f32[4,128,128]{2,1,0:T(8,128)} %copy-done.3), custom_call_target="InvertDiagBlocksLowerTriangular" | custom-call | tf_op jit(solution)/shard_map/jit(_solve_triangular)/triangular_solve | solution.py:16
  204.7 17.3 %select_bitcast_fusion = f32[4096,512]{0,1:T(8,128)} fusion(f32[4096,512]{1,0:T(8,128)} %bitcast.119, pred[4096]{0:T(1024)(128)(4,1)S(1)} %bitcast.122, pred[]{:T(512)S(6)} %eq.29, f32[128,512]{1,0:T(8,128)S(1)} %fusion.64, f32[128,512]{1,0:T(8,128)S(1)} %fusion.65, f32[128,512]{1,0:T(8,128)S(1)} %fusion.67, f32[128,512]{1,0:T(8,128)S(1)} %fusion.42), kind=kOutput, calls=%fused_computation.5 | convolution fusion | flops 12889882624 | bytes 17829888 | tf_op jit(solution)/shard_map/dot_general | solution.py:17
  222.1 123.9 %all-reduce.10.cloned.1.call-done = f32[4096,512]{0,1:T(8,128)} async-done(((f32[4096,512]{0,1:T(8,128)}), f32[4096,512]{0,1:T(8,128)}) %all-reduce.10.cloned.1.call-update) | async-done | bytes 8388624 | tf_op jit(solution)/shard_map/psum | solution.py:11
  348.8 9.0 %copy.5 = f32[4096,512]{1,0:T(8,128)} copy(f32[4096,512]{0,1:T(8,128)} %all-reduce.10.cloned.1.call-done) | data formatting | bytes 16777216 | tf_op jit(solution)/shard_map/psum | solution.py:11
  357.8 34.2 %all-reduce.12.cloned.1.call-done = f32[512,512]{0,1:T(8,128)} async-done(((f32[512,512]{0,1:T(8,128)}), f32[512,512]{0,1:T(8,128)}) %all-reduce.12.cloned.1.call-update) | async-done | bytes 1048592 | tf_op jit(solution)/shard_map/psum | solution.py:11
  392.0 24.0 %broadcast_select_fusion = (f32[4096,512]{1,0:T(8,128)}, f32[4096,512]{1,0:T(8,128)}) fusion(f32[4096,512]{1,0:T(8,128)} %copy.5, pred[4096]{0:T(1024)(128)(4,1)S(1)} %bitcast.123, f32[4096,512]{1,0:T(8,128)} %bitcast.120, f32[4096,512]{0,1:T(8,128)} %all-reduce.10.cloned.1.call-done, f32[512,512]{0,1:T(8,128)} %all-reduce.12.cloned.1.call-done), kind=kOutput, calls=%fused_computation.8 | convolution fusion | flops 12889096192 | bytes 42995712 | tf_op jit(solution)/shard_map/dot_general | solution.py:58
  418.4 9.0 %broadcast_select_fusion.2 = f32[4096,512]{1,0:T(8,128)} fusion(f32[4096,512]{1,0:T(8,128)} %fusion.2, f32[4096,512]{1,0:T(8,128)} %get-tuple-element.156, pred[]{:T(512)S(6)} %eq.29), kind=kLoop, calls=%fused_computation.10 | loop fusion | flops 2097152 | bytes 25165824 | tf_op jit(solution)/shard_map/jit(_where)/select_n | solution.py:73
  431.6 46.5 %all-reduce.14.cloned.1.call-done = f32[512,512]{0,1:T(8,128)} async-done(((f32[512,512]{0,1:T(8,128)}), f32[512,512]{0,1:T(8,128)}) %all-reduce.14.cloned.1.call-update) | async-done | bytes 1048592 | tf_op jit(solution)/shard_map/psum | solution.py:11
  481.1 11.7 %cholesky.358 = f32[128,128]{1,0:T(8,128)S(1)} custom-call(f32[128,128]{1,0:T(8,128)S(1)} %cholesky.439), custom_call_target="Cholesky" | custom-call | tf_op jit(solution)/shard_map/jit(cholesky)/cholesky | solution.py:15
  493.0 9.8 %custom-call.31 = f32[1,128,128]{1,2,0:T(8,128)S(1)} custom-call(f32[1,128,128]{2,1,0:T(8,128)S(1)} %get-tuple-element.142), custom_call_target="InvertDiagBlocksLowerTriangular" | custom-call | tf_op jit(solution)/shard_map/jit(cholesky)/cholesky | solution.py:15
  503.4 11.7 %cholesky.377 = f32[128,128]{1,0:T(8,128)S(1)} custom-call(f32[128,128]{1,0:T(8,128)S(1)} %cholesky.443), custom_call_target="Cholesky" | custom-call | tf_op jit(solution)/shard_map/jit(cholesky)/cholesky | solution.py:15
  516.5 10.0 %custom-call.32 = f32[1,128,128]{1,2,0:T(8,128)S(1)} custom-call(f32[1,128,128]{2,1,0:T(8,128)S(1)} %get-tuple-element.139), custom_call_target="InvertDiagBlocksLowerTriangular" | custom-call | tf_op jit(solution)/shard_map/jit(cholesky)/cholesky | solution.py:15
  527.2 11.7 %cholesky.398 = f32[128,128]{1,0:T(8,128)S(1)} custom-call(f32[128,128]{1,0:T(8,128)S(1)} %cholesky.448), custom_call_target="Cholesky" | custom-call | tf_op jit(solution)/shard_map/jit(cholesky)/cholesky | solution.py:15
  539.6 9.8 %custom-call.33 = f32[1,128,128]{1,2,0:T(8,128)S(1)} custom-call(f32[1,128,128]{2,1,0:T(8,128)S(1)} %get-tuple-element.136), custom_call_target="InvertDiagBlocksLowerTriangular" | custom-call | tf_op jit(solution)/shard_map/jit(cholesky)/cholesky | solution.py:15
  550.0 11.7 %cholesky.415 = f32[128,128]{1,0:T(8,128)S(1)} custom-call(f32[128,128]{1,0:T(8,128)S(1)} %convolution_subtract_fusion.12), custom_call_target="Cholesky" | custom-call | tf_op jit(solution)/shard_map/jit(cholesky)/cholesky | solution.py:15
  565.6 8.1 while.13
  574.4 40.1 %custom-call.34 = f32[4,128,128]{1,2,0:T(8,128)S(1)} custom-call(f32[4,128,128]{2,1,0:T(8,128)} %copy-done.2), custom_call_target="InvertDiagBlocksLowerTriangular" | custom-call | tf_op jit(solution)/shard_map/jit(_solve_triangular)/triangular_solve | solution.py:16
  617.7 18.0 %select_select_fusion = f32[4096,512]{1,0:T(8,128)} fusion(f32[4096,512]{1,0:T(8,128)} %get-tuple-element.127, pred[4096]{0:T(1024)(128)(4,1)S(1)} %bitcast.124, pred[]{:T(512)S(6)} %eq.28, f32[128,512]{1,0:T(8,128)S(1)} %fusion.58, f32[128,512]{1,0:T(8,128)S(1)} %fusion.59, f32[128,512]{1,0:T(8,128)S(1)} %fusion.61, f32[128,512]{1,0:T(8,128)S(1)} %fusion.40), kind=kOutput, calls=%fused_computation.4 | convolution fusion | flops 12889882624 | bytes 17829888 | tf_op jit(solution)/shard_map/dot_general | solution.py:17
  636.0 123.8 %all-reduce.16.cloned.1.call-done = f32[4096,512]{1,0:T(8,128)} async-done(((f32[4096,512]{1,0:T(8,128)}), f32[4096,512]{1,0:T(8,128)}) %all-reduce.16.cloned.1.call-update) | async-done | bytes 8388624 | tf_op jit(solution)/shard_map/psum | solution.py:11
  762.6 43.6 %all-reduce.18.cloned.1.call-done = f32[512,512]{0,1:T(8,128)} async-done(((f32[512,512]{0,1:T(8,128)}), f32[512,512]{0,1:T(8,128)}) %all-reduce.18.cloned.1.call-update) | async-done | bytes 1048592 | tf_op jit(solution)/shard_map/psum | solution.py:11
  806.3 24.8 %broadcast_select_fusion.1 = (f32[4096,512]{1,0:T(8,128)}, f32[4096,512]{1,0:T(8,128)}) fusion(f32[4096,512]{1,0:T(8,128)} %all-reduce.16.cloned.1.call-done, pred[4096]{0:T(1024)(128)(4,1)S(1)} %bitcast.125, f32[4096,512]{1,0:T(8,128)} %get-tuple-element.127, f32[512,512]{0,1:T(8,128)} %all-reduce.18.cloned.1.call-done), kind=kOutput, calls=%fused_computation.9 | convolution fusion | flops 12889096192 | bytes 34607104 | tf_op jit(solution)/shard_map/dot_general | solution.py:58
  833.4 8.8 %broadcast_select_fusion.3 = f32[4096,512]{1,0:T(8,128)} fusion(f32[4096,512]{1,0:T(8,128)} %fusion.1, f32[4096,512]{1,0:T(8,128)} %get-tuple-element.160, pred[]{:T(512)S(6)} %eq.28), kind=kLoop, calls=%fused_computation.11 | loop fusion | flops 2097152 | bytes 25165824 | tf_op jit(solution)/shard_map/jit(_where)/select_n | solution.py:73
  844.6 10.9 %copy.11 = f32[1,8,512,1,1,512]{5,4,3,2,1,0:T(1,128)} copy(f32[1,8,512,1,1,512]{5,2,1,4,3,0:T(8,128)} %bitcast.121) | data formatting | bytes 16777216 | tf_op jit(solution)/shard_map/reshape | solution.py:79
  (124 shorter events, 69.2 us)
Async XLA Ops:
  6.5 50.8 %all-reduce.8.cloned.1.call-start = ((), (), s32[]{:S(2)}) async-start(), calls=%async_computation | async-start | bytes 2097152 | tf_op jit(solution)/shard_map/psum | solution.py:11
  11.0 335.0 %all-reduce.10.cloned.1.call-start = ((), (), s32[]{:S(2)}) async-start(), calls=%async_computation.1 | async-start | bytes 16777216 | tf_op jit(solution)/shard_map/psum | solution.py:11
  160.7 0.7 copy-start.3
  222.0 170.1 %all-reduce.12.cloned.1.call-start = ((), (), s32[]{:S(2)}) async-start(), calls=%async_computation.2 | async-start | bytes 2097152 | tf_op jit(solution)/shard_map/psum | solution.py:11
  348.4 129.7 %all-reduce.14.cloned.1.call-start = ((), (), s32[]{:S(2)}) async-start(), calls=%async_computation.3 | async-start | bytes 2097152 | tf_op jit(solution)/shard_map/psum | solution.py:11
  418.4 9.0 %copy-start = (f32[512,512]{0,1:T(8,128)S(1)}, f32[512,512]{0,1:T(8,128)}, u32[]{:S(2)}) copy-start(f32[512,512]{0,1:T(8,128)} %all-reduce.12.cloned.1.call-done) | copy-start | bytes 3145732
  431.3 328.5 %all-reduce.16.cloned.1.call-start = ((), (), s32[]{:S(2)}) async-start(), calls=%async_computation.4 | async-start | bytes 16777216 | tf_op jit(solution)/shard_map/psum | solution.py:11
  573.7 0.7 copy-start.2
  635.7 170.5 %all-reduce.18.cloned.1.call-start = ((), (), s32[]{:S(2)}) async-start(), calls=%async_computation.5 | async-start | bytes 2097152 | tf_op jit(solution)/shard_map/psum | solution.py:11
  833.4 8.8 %copy-start.1 = (f32[512,512]{0,1:T(8,128)S(1)}, f32[512,512]{0,1:T(8,128)}, u32[]{:S(2)}) copy-start(f32[512,512]{0,1:T(8,128)} %all-reduce.18.cloned.1.call-done) | copy-start | bytes 3145732
Sparse Core Ops, SparseCore 0:
  11.1 46.1 all-reduce.7
  222.1 123.8 all-reduce.9
  348.5 43.4 all-reduce.11
  431.4 46.6 all-reduce.13
  635.9 123.8 all-reduce.15
  762.7 43.4 all-reduce.17
where the time goes:
time: 870 us; the launch traced here: 863 us
  waiting for transfers between devices  410 us (47%)
  other arithmetic  284 us (33%)
  matrix products  94 us (11%)
  local copies, waits for them, and re-layouts  54 us (6%)
  between operations  19.2 us (2%)
    psum x6, waiting for transfers between devices, broadcast(): return lax.psum(kept, axis)  410 us
    another operation x29, other arithmetic, solve_panel(): factor = jnp.tril(jnp.linalg.cholesky(corner))  167 us
    another operation x5, other arithmetic, solve_panel(): inverse = jax.scipy.linalg.solve_triangular(factor, eye, lower=True)  80.9 us
    dot_general x2, matrix products, body(): lax.dot_general(panel, pieces, (((1,), (1,)), ((), ())), precision=lax.Pr...  48.7 us
    dot_general x2, matrix products, solve_panel(): lax.dot_general(column, inverse, (((1,), (1,)), ((), ())), precision=lax....  35.3 us
    select_n x2, other arithmetic, body(): column_new = jnp.where(owns_column, column_new, column_now)  17.8 us
  transfers between devices with their start and end apart: 6, of which 6 were waited for; matrix products, arithmetic and copies ran while one was open for 2% of the time, Pallas kernels for 0%

commit v1 on v0

v1 whole, which is shorter than its diff:
```python
import jax
import jax.numpy as jnp
from jax import lax
from jax.experimental import pallas as pl
from jax.experimental.pallas import tpu as pltpu
from jax.sharding import PartitionSpec as P
HI = lax.Precision.HIGHEST
T = 128
NT = 8
NB = 512
N2 = 1024


def dot(a, b, ca=1, cb=0):
    return lax.dot_general(a, b, (((ca,), (cb,)), ((), ())), precision=HI, preferred_element_type=jnp.float32)


def sub_bcast(x, j):
    return jnp.broadcast_to(x[j : j + 1, :], (8, T))


def lane_bcast(x, j):
    return jnp.broadcast_to(x[:, j : j + 1], (8, T))


def factor_tile(rows):
    sub = lax.broadcasted_iota(jnp.int32, (8, T), 0)
    lane = lax.broadcasted_iota(jnp.int32, (8, T), 1)
    inv_rows, fac_rows = [], []
    for b in range(T // 8):
        r0 = 8 * b
        low = rows[b]
        full = rows[b]
        cols = [lane_bcast(rows[b], r0 + j) for j in range(8)]
        later = {i: [lane_bcast(rows[i], r0 + j) for j in range(8)] for i in range(b + 1, T // 8)}
        dvec = jnp.zeros((8, T), jnp.float32)
        rvec = jnp.zeros((8, T), jnp.float32)
        for j in range(8):
            d = sub_bcast(cols[j], j)
            rinv = 1.0 / d
            f = cols[j] * rinv
            here = lane == r0 + j
            fg = jnp.where(sub == j, 0.0, f)
            fl = jnp.where(sub > j, f, 0.0)
            for jj in range(j + 1, 8):
                cols[jj] = cols[jj] - fg * sub_bcast(cols[jj], j)
            low_now = jnp.where(here & (sub > j), 0.0, low)
            lrow = jnp.where(here, 1.0, sub_bcast(low, j))
            low = low_now - fl * lrow
            grow = jnp.where(here, 1.0, sub_bcast(full, j))
            full = jnp.where(here, jnp.where(sub == j, 1.0, 0.0), full) - fg * grow
            dvec = jnp.where(sub == j, d, dvec)
            rvec = jnp.where(sub == j, rinv, rvec)
        full = full * rvec
        pieces = [sub_bcast(full, j) for j in range(8)]
        inblk = (lane >= r0) & (lane < r0 + 8)
        for i in range(b + 1, T // 8):
            acc = jnp.where(inblk, 0.0, rows[i])
            for j in range(8):
                acc = acc - later[i][j] * pieces[j]
            rows[i] = acc
        rs = lax.rsqrt(dvec)
        rs = rs * (1.5 - 0.5 * dvec * rs * rs)
        row = sub + r0
        scaled = low * rs
        inv_rows.append(jnp.where(lane < row, scaled, jnp.where(lane == row, rs, 0.0)))
        fac_rows.append(jnp.where(lane >= row, scaled, 0.0))
    return inv_rows, fac_rows


def factor_kernel(s_ref, b_ref, top_ref, q_ref, m, u_ref, g_ref, w_ref):
    pr = lax.axis_index("pr")
    pc = lax.axis_index("pc")
    m[0:NB, 0:NB] = s_ref[0]
    m[0:NB, NB:] = s_ref[1]
    m[NB:, NB:] = s_ref[2]

    @pl.loop(0, NT)
    def _(t):
        o = pl.multiple_of(t * T, T)
        rows = [m[pl.ds(o + 8 * i, 8), pl.ds(o, T)] for i in range(T // 8)]
        inv_rows, fac_rows = factor_tile(rows)
        for i in range(T // 8):
            g_ref[pl.ds(o + 8 * i, 8), :] = inv_rows[i]
            u_ref[pl.ds(o + 8 * i, 8), pl.ds(o, T)] = fac_rows[i]
        for ts in range(NT - 1):

            @pl.when(t == ts)
            def _():
                a, b = ts * T, (ts + 1) * T
                u = dot(g_ref[a:b, :], m[a:b, b:])
                u_ref[a:b, b:] = u
                for i in range(ts + 1, NT):
                    lo = (i - ts - 1) * T
                    m[i * T : (i + 1) * T, i * T :] -= dot(u[:, lo : lo + T], u[:, lo:], 0, 0)

    for t in range(NT):
        a, b = t * T, (t + 1) * T
        acc = b_ref[a:b, :]
        if t:
            acc = acc - dot(u_ref[0:a, a:b], w_ref[0:a, :], 0, 0)
        w_ref[a:b, :] = dot(g_ref[a:b, :], acc)

    top_ref[...] = w_ref[pl.ds(pl.multiple_of(jnp.minimum(pr, 1) * NB, NB), NB), :]
    for k in range(2):

        @pl.when((pc == k) & (pr == k))
        def _():
            for i in range(NB // T):
                for j in range(NB // T):
                    a, b = k * NB + i * T, k * NB + j * T
                    if j <= i:
                        piece = u_ref[b : b + T, a : a + T].T
                    else:
                        piece = jnp.zeros((T, T), jnp.float32)
                    top_ref[i * T : (i + 1) * T, j * T : (j + 1) * T] = piece

    @pl.when(pc < 2)
    def _():
        row = lax.broadcasted_iota(jnp.int32, (N2, NB), 0)
        col = lax.broadcasted_iota(jnp.int32, (N2, NB), 1)
        w_ref[...] = jnp.where(row == col + pc * NB, -1.0, 0.0)

    for t in reversed(range(NT)):
        a, b = t * T, (t + 1) * T
        acc = w_ref[a:b, :]
        if t < NT - 1:
            acc = acc - dot(u_ref[a:b, b:], q_ref[b:, :])
        q_ref[a:b, :] = dot(g_ref[a:b, :], acc, 0, 0)


def factor(s, b):
    vmem = pl.BlockSpec(memory_space=pltpu.VMEM)
    return pl.pallas_call(
        factor_kernel,
        out_shape=(jax.ShapeDtypeStruct((NB, NB), jnp.float32), jax.ShapeDtypeStruct((N2, NB), jnp.float32)),
        in_specs=[vmem, vmem],
        out_specs=(vmem, vmem),
        scratch_shapes=[
            pltpu.VMEM((N2, N2), jnp.float32),
            pltpu.VMEM((N2, N2), jnp.float32),
            pltpu.VMEM((N2, T), jnp.float32),
            pltpu.VMEM((N2, NB), jnp.float32),
        ],
        compiler_params=pltpu.CompilerParams(vmem_limit_bytes=48 << 20),
        cost_estimate=pl.CostEstimate(flops=40_000_000_000, bytes_accessed=10_000_000, transcendentals=0),
    )(s, b)


def split(x):
    hi = x.astype(jnp.bfloat16)
    return hi, (x - hi.astype(jnp.float32)).astype(jnp.bfloat16)


def mm(a, b):
    return lax.dot_general(a, b, (((1,), (0,)), ((), ())), preferred_element_type=jnp.float32)


def update_kernel(a_ref, p_ref, q_ref, top_ref, o_ref, qh, ql):
    l = pl.program_id(0)
    pr = lax.axis_index("pr")
    pc = lax.axis_index("pc")

    @pl.when(l == 0)
    def _():
        qh[...], ql[...] = split(q_ref[...])

    keep = jnp.where(pc < 2, 0.0, 1.0)
    acc = None
    for k in range(2):
        ph, plo = split(p_ref[:, k].reshape(NB, NB))
        h, lo = qh[k * NB : (k + 1) * NB], ql[k * NB : (k + 1) * NB]
        part = mm(ph, h) + (mm(ph, lo) + mm(plo, h))
        acc = part if acc is None else acc + part
    for c in range(4):
        at = pl.ds(c, NB, stride=4)
        o_ref[at, :] = keep * a_ref[at, :] - acc[:, c * T : (c + 1) * T]

    @pl.when((l == 0) & ((pr == 0) | ((pr == 1) & (pc > 0))))
    def _():
        for c in range(4):
            o_ref[pl.ds(c, NB, stride=4), :] = top_ref[:, c * T : (c + 1) * T]


def update(a, p, q, top):
    return pl.pallas_call(
        update_kernel,
        grid=(8,),
        out_shape=jax.ShapeDtypeStruct(a.shape, jnp.float32),
        in_specs=[
            pl.BlockSpec((4 * NB, T), lambda l: (l, 0)),
            pl.BlockSpec((4, 2, T, NB), lambda l: (l, 0, 0, 0)),
            pl.BlockSpec((N2, NB), lambda l: (0, 0)),
            pl.BlockSpec((NB, NB), lambda l: (0, 0)),
        ],
        out_specs=pl.BlockSpec((4 * NB, T), lambda l: (l, 0)),
        scratch_shapes=[pltpu.VMEM((N2, NB), jnp.bfloat16), pltpu.VMEM((N2, NB), jnp.bfloat16)],
        compiler_params=pltpu.CompilerParams(vmem_limit_bytes=48 << 20),
        cost_estimate=pl.CostEstimate(flops=13_000_000_000, bytes_accessed=34_000_000, transcendentals=0),
    )(a, p, q, top)


def body(matrix):
    flat = matrix.reshape(8 * NB * 4, T)
    first = matrix[0, 0].reshape(NB, NB)
    pr = lax.axis_index("pr")
    pc = lax.axis_index("pc")
    owner = [(pr == 0) & (pc == 0), (pr == 0) & (pc == 1), (pr == 1) & (pc == 1)]
    s = lax.psum(jnp.stack([jnp.where(o, first, 0.0) for o in owner]), ("pr", "pc"))
    b = lax.all_gather(first, "pr")[:2].reshape(N2, NB)
    turned = first.T
    mine = []
    for k in range(2):
        got = None
        for part in range(4):
            pairs = [(k * 32 + i, (i % 4) * 32 + 4 * (i // 4) + part) for i in range(32)]
            one = lax.ppermute(turned[part * T : (part + 1) * T], ("pr", "pc"), pairs)
            got = one if got is None else got + one
        mine.append(got)
    panel = lax.all_gather(jnp.stack(mine), "pc")
    top, q = factor(s, b)
    return update(flat, panel, q, top).reshape(matrix.shape)


def solution(mesh):
    return jax.shard_map(
        body,
        mesh=mesh,
        in_specs=(P("pr", None, None, "pc", None, None),),
        out_specs=P("pr", None, None, "pc", None, None),
        check_vma=False,
    )
```

time: 870 us -> 328 us (0.38)
  other arithmetic: 284 us -> 5.6 us
  waiting for transfers between devices: 410 us -> 210 us
  matrix products: 94 us -> 0 us
  Pallas kernels: 0 us -> 81 us
  local copies, waits for them, and re-layouts: 54 us -> 7.78 us
    another operation x34 -> x4, other arithmetic: 248 us -> 3.48 us  [the longest x1 3.29 us: body(): jnp.stack([jnp.where(o, first, 0.0) for o in owner])]
    psum x6 -> x1, waiting for transfers between devices: 410 us -> 171 us  [body(): lax.psum(jnp.stack([jnp.where(o, first, 0.0) for o in owner]), ('pr', 'pc'))]
    dot_general x4 -> x0, matrix products: 84 us -> none  [the longest x2 48.7 us: body(): lax.dot_general(panel, pieces, (((1,), (1,)), ((), ())), precision=lax.Pr...]
    pallas_call x0 -> x2, Pallas kernels: none -> 81 us  [the longest x1 61.7 us: factor(): pl.pallas_call(factor_kernel, out_shape=(jax.ShapeDtypeStruct((NB, NB), j...]
    select_n x6 -> x0, other arithmetic: 23.5 us -> none  [the longest x2 17.8 us: body(): column_new = jnp.where(owns_column, column_new, column_now)]
    all_gather x0 -> x2, waiting for transfers between devices: none -> 19.7 us  [the longest x1 19.7 us: body(): b = lax.all_gather(first, 'pr')[:2].reshape(N2, NB)]
    ppermute x0 -> x8, waiting for transfers between devices: none -> 19.1 us  [body(): one = lax.ppermute(turned[part * T:(part + 1) * T], ('pr', 'pc'), pairs)]
    another operation x35 -> x1, local copies, waits for them, and re-layouts: 16.4 us -> 1.04 us  [body(): panel = lax.all_gather(jnp.stack(mine), 'pc')]
  transfers between devices with their start and end apart: 6 -> 11, of which waited for: 6 -> 4; matrix products, arithmetic and copies ran while one was open for 2% -> 2% of each run, Pallas kernels for 0% -> 19%
where the time goes in v1:
time: 328 us; the launch traced here: 326 us
  waiting for transfers between devices  210 us (64%)
  Pallas kernels  81 us (25%)
  between operations  15 us (5%)
  local copies, waits for them, and re-layouts  7.78 us (2%)
  starting transfers between devices  6.9 us (2%)
  other arithmetic  5.6 us (2%)
    psum x1, waiting for transfers between devices, body(): lax.psum(jnp.stack([jnp.where(o, first, 0.0) for o in owner]), ('pr', 'pc'))  171 us
    pallas_call x1, Pallas kernels, factor(): pl.pallas_call(factor_kernel, out_shape=(jax.ShapeDtypeStruct((NB, NB), j...  61.7 us
    all_gather x1, waiting for transfers between devices, body(): b = lax.all_gather(first, 'pr')[:2].reshape(N2, NB)  19.7 us
    pallas_call x1, Pallas kernels, update(): pl.pallas_call(update_kernel, grid=(8,), out_shape=jax.ShapeDtypeStruct(a...  19.4 us
    ppermute x8, waiting for transfers between devices, body(): one = lax.ppermute(turned[part * T:(part + 1) * T], ('pr', 'pc'), pairs)  19.1 us
    ppermute x8, starting transfers between devices, body(): one = lax.ppermute(turned[part * T:(part + 1) * T], ('pr', 'pc'), pairs)  6.82 us
  transfers between devices with their start and end apart: 11, of which 4 were waited for; matrix products, arithmetic and copies ran while one was open for 2% of the time, Pallas kernels for 19%

profile of v1, /device:TPU:7, one launch (start us, length us, event | category | flops | bytes accessed | tf_op | source)
XLA Modules:
  0.0 326.1 jit_solution(12091341993167926388)
XLA Ops:
  7.4 1.9 slice.22
  9.3 2.1 fusion
  11.4 0.0 all-gather.7.cloned.1.call-update
  11.5 0.0 all-reduce.2.cloned.1.call-start
  11.5 3.3 %pad_maximum_fusion = f32[3,512,512]{2,1,0:T(8,128)} fusion(f32[1,512,512]{2,1,0:T(8,128)S(1)} %get-tuple-element.11, f32[1,512,512]{2,1,0:T(8,128)} %get-tuple-element.13, f32[1,512,512]{2,1,0:T(8,128)S(1)} %get-tuple-element.12), kind=kLoop, calls=%fused_computation | loop fusion | flops 1572864 | bytes 6291456 | tf_op jit(solution)/shard_map/stack | solution.py:209
  14.8 0.0 all-reduce.2.cloned.1.call-update
  14.8 0.0 all-gather.5.cloned.1.call-start
  14.9 0.1 fusion.1
  15.0 1.3 collective-permute-start.5
  16.3 0.7 collective-permute-start.7
  16.9 0.7 collective-permute-start.6
  17.6 0.7 collective-permute-start.4
  18.3 1.3 collective-permute-start.1
  19.6 4.9 %collective-permute-done.5 = f32[128,512]{0,1:T(8,128)S(1)} collective-permute-done((f32[128,512]{0,1:T(8,128)S(1)}, f32[128,512]{0,1:T(8,128)S(1)}, u32[]{:S(2)}, u32[]{:S(2)}) %collective-permute-start.5) | collective-permute-done | bytes 262176 | tf_op jit(solution)/shard_map/ppermute | solution.py:217
  24.5 0.7 collective-permute-start.3
  25.1 0.0 collective-permute-done.7
  25.2 0.7 collective-permute-start.2
  25.9 0.9 collective-permute-start
  26.7 0.0 collective-permute-done.4
  26.7 0.1 add_bitcast_fusion
  26.8 14.2 %collective-permute-done.1 = f32[128,512]{0,1:T(8,128)S(1)} collective-permute-done((f32[128,512]{0,1:T(8,128)S(1)}, f32[128,512]{0,1:T(8,128)S(1)}, u32[]{:S(2)}, u32[]{:S(2)}) %collective-permute-start.1) | collective-permute-done | bytes 262176 | tf_op jit(solution)/shard_map/ppermute | solution.py:217
  41.1 0.1 add_bitcast_fusion.1
  41.2 1.0 copy.6
  42.2 0.0 all-gather.5.cloned.1.call-update
  42.3 19.7 %all-gather.7.cloned.1.call-done = f32[4,1,512,1,1,512]{5,2,4,3,1,0:T(8,128)} async-done(((f32[1,1,512,1,1,512]{5,2,4,3,1,0:T(8,128)}), f32[4,1,512,1,1,512]{5,2,4,3,1,0:T(8,128)}) %all-gather.7.cloned.1.call-update) | async-done | bytes 4194320 | tf_op jit(solution)/shard_map/all_gather | solution.py:210
  61.9 1.8 slice.33
  63.7 171.0 %all-reduce.2.cloned.1.call-done.s_ref = f32[3,512,512]{2,1,0:T(8,128)} async-done(((f32[3,512,512]{2,1,0:T(8,128)}), f32[3,512,512]{2,1,0:T(8,128)}) %all-reduce.2.cloned.1.call-update) | async-done | bytes 3145744 | tf_op jit(solution)/shard_map/psum | solution.py:209
  234.7 61.7 %shard_map.17 = (f32[512,512]{1,0:T(8,128)S(1)}, f32[1024,512]{1,0:T(8,128)S(1)}) custom-call(f32[3,512,512]{2,1,0:T(8,128)} %all-reduce.2.cloned.1.call-done.s_ref, f32[1024,512]{1,0:T(8,128)S(1)} %bitcast.18), custom_call_target="tpu_custom_call" | custom-call | flops 40000000000 | bytes 10000000 | tf_op jit(solution)/shard_map/pallas_call | solution.py:134
  296.4 0.0 copy-start
  296.4 1.3 copy-done
  297.7 1.6 copy-done.1
  299.3 19.4 %shard_map.18 = f32[16384,128]{1,0:T(8,128)} custom-call(f32[16384,128]{1,0:T(8,128)} %bitcast.19, f32[32,2,128,512]{3,2,1,0:T(8,128)} %bitcast.20, f32[1024,512]{1,0:T(8,128)S(1)} %copy-done.1, f32[512,512]{1,0:T(8,128)S(1)} %get-tuple-element.8.top_ref), custom_call_target="tpu_custom_call" | custom-call | flops 12999999488 | bytes 34000000 | tf_op jit(solution)/shard_map/pallas_call | solution.py:186
  (8 shorter events, 0.1 us)
Async XLA Ops:
  7.4 54.5 %all-gather.7.cloned.1.call-start = ((), (), s32[]{:S(2)}) async-start(), calls=%async_computation.2 | async-start | bytes 5242880 | tf_op jit(solution)/shard_map/all_gather | solution.py:210
  11.5 223.2 %all-reduce.2.cloned.1.call-start = ((), (), s32[]{:S(2)}) async-start(), calls=%async_computation | async-start | bytes 6291456 | tf_op jit(solution)/shard_map/psum | solution.py:209
  14.8 282.9 %all-gather.5.cloned.1.call-start = ((), (), s32[]{:S(2)}) async-start(), calls=%async_computation.1 | async-start | bytes 17301504 | tf_op jit(solution)/shard_map/all_gather | solution.py:220
  15.0 9.5 %collective-permute-start.5 = (f32[128,512]{0,1:T(8,128)S(1)}, f32[128,512]{0,1:T(8,128)S(1)}, u32[]{:S(2)}, u32[]{:S(2)}) collective-permute-start(f32[128,512]{0,1:T(8,128)S(1)} %get-tuple-element.14), channel_id=1, source_target_pairs={{32,1},{33,33},{34,65},{35,97},{36,5},{37,37},{38,69},{39,101},{40... | collective-permute-start | bytes 786440 | tf_op jit(solution)/shard_map/ppermute | solution.py:217
  16.3 8.9 %collective-permute-start.7 = (f32[128,512]{0,1:T(8,128)S(1)}, f32[128,512]{0,1:T(8,128)S(1)}, u32[]{:S(2)}, u32[]{:S(2)}) collective-permute-start(f32[128,512]{0,1:T(8,128)S(1)} %get-tuple-element.15), channel_id=1, source_target_pairs={{32,3},{33,35},{34,67},{35,99},{36,7},{37,39},{38,71},{39,103},{40... | collective-permute-start | bytes 786440 | tf_op jit(solution)/shard_map/ppermute | solution.py:217
  16.9 8.9 %collective-permute-start.6 = (f32[128,512]{0,1:T(8,128)S(1)}, f32[128,512]{0,1:T(8,128)S(1)}, u32[]{:S(2)}, u32[]{:S(2)}) collective-permute-start(f32[128,512]{0,1:T(8,128)S(1)} %get-tuple-element.16), channel_id=1, source_target_pairs={{32,2},{33,34},{34,66},{35,98},{36,6},{37,38},{38,70},{39,102},{40... | collective-permute-start | bytes 786440 | tf_op jit(solution)/shard_map/ppermute | solution.py:217
  17.6 9.1 %collective-permute-start.4 = (f32[128,512]{0,1:T(8,128)S(1)}, f32[128,512]{0,1:T(8,128)S(1)}, u32[]{:S(2)}, u32[]{:S(2)}) collective-permute-start(f32[128,512]{0,1:T(8,128)S(1)} %get-tuple-element.17), channel_id=1, source_target_pairs={{32,0},{33,32},{34,64},{35,96},{36,4},{37,36},{38,68},{39,100},{40... | collective-permute-start | bytes 786440 | tf_op jit(solution)/shard_map/ppermute | solution.py:217
  18.3 22.7 %collective-permute-start.1 = (f32[128,512]{0,1:T(8,128)S(1)}, f32[128,512]{0,1:T(8,128)S(1)}, u32[]{:S(2)}, u32[]{:S(2)}) collective-permute-start(f32[128,512]{0,1:T(8,128)S(1)} %get-tuple-element.14), channel_id=1, source_target_pairs={{0,1},{1,33},{2,65},{3,97},{4,5},{5,37},{6,69},{7,101},{8,9},{9,41... | collective-permute-start | bytes 786440 | tf_op jit(solution)/shard_map/ppermute | solution.py:217
  24.5 16.6 %collective-permute-start.3 = (f32[128,512]{0,1:T(8,128)S(1)}, f32[128,512]{0,1:T(8,128)S(1)}, u32[]{:S(2)}, u32[]{:S(2)}) collective-permute-start(f32[128,512]{0,1:T(8,128)S(1)} %get-tuple-element.15), channel_id=1, source_target_pairs={{0,3},{1,35},{2,67},{3,99},{4,7},{5,39},{6,71},{7,103},{8,11},{9,4... | collective-permute-start | bytes 786440 | tf_op jit(solution)/shard_map/ppermute | solution.py:217
  25.2 15.9 %collective-permute-start.2 = (f32[128,512]{0,1:T(8,128)S(1)}, f32[128,512]{0,1:T(8,128)S(1)}, u32[]{:S(2)}, u32[]{:S(2)}) collective-permute-start(f32[128,512]{0,1:T(8,128)S(1)} %get-tuple-element.16), channel_id=1, source_target_pairs={{0,2},{1,34},{2,66},{3,98},{4,6},{5,38},{6,70},{7,102},{8,10},{9,4... | collective-permute-start | bytes 786440 | tf_op jit(solution)/shard_map/ppermute | solution.py:217
  25.9 15.2 %collective-permute-start = (f32[128,512]{0,1:T(8,128)S(1)}, f32[128,512]{0,1:T(8,128)S(1)}, u32[]{:S(2)}, u32[]{:S(2)}) collective-permute-start(f32[128,512]{0,1:T(8,128)S(1)} %get-tuple-element.17), channel_id=1, source_target_pairs={{0,0},{1,32},{2,64},{3,96},{4,4},{5,36},{6,68},{7,100},{8,8},{9,40... | collective-permute-start | bytes 786440 | tf_op jit(solution)/shard_map/ppermute | solution.py:217
  296.4 1.3 copy-start
  297.7 1.6 copy-start.1
Sparse Core Ops, SparseCore 0:
  11.6 50.2 all-gather.6
  64.2 91.9 all-gather.4
Sparse Core Ops, SparseCore 1:
  16.7 218.0 all-reduce.1

commit v2 on v1

--- a/solution.py
+++ b/solution.py
@@ -9,6 +9,8 @@
 NT = 8
 NB = 512
 N2 = 1024
+MESH = pl.DeviceIdType.MESH
+ROOTS = ((0, 0), (0, 1), (1, 1))
 
 
 def dot(a, b, ca=1, cb=0):
@@ -68,49 +70,282 @@
     return inv_rows, fac_rows
 
 
-def factor_kernel(s_ref, b_ref, top_ref, q_ref, m, u_ref, g_ref, w_ref):
-    pr = lax.axis_index("pr")
-    pc = lax.axis_index("pc")
-    m[0:NB, 0:NB] = s_ref[0]
-    m[0:NB, NB:] = s_ref[1]
-    m[NB:, NB:] = s_ref[2]
+class Links:
+    def __init__(self, a, sbuf, bbuf, local, scat_s, scat_r, x_s, x_r, ag_s, ag_r, b_s, b_r):
+        self.a, self.sbuf, self.bbuf, self.local = a, sbuf, bbuf, local
+        self.scat_s, self.scat_r, self.x_s, self.x_r = scat_s, scat_r, x_s, x_r
+        self.ag_s, self.ag_r, self.b_s, self.b_r = ag_s, ag_r, b_s, b_r
+        self.pr, self.pc = lax.axis_index("pr"), lax.axis_index("pc")
+        self.y, self.z, self.c = self.pc // 8, (self.pc // 2) % 4, self.pc % 2
+
+    def copy(self, src, dst, send, recv, pr, pc):
+        return pltpu.make_async_remote_copy(
+            src_ref=src, dst_ref=dst, send_sem=send, recv_sem=recv, device_id={"pr": pr, "pc": pc}, device_id_type=MESH
+        )
+
+    def place(self, y, z, c):
+        return (y * 4 + z) * 2 + c
+
+    def barrier(self):
+        sem = pltpu.get_barrier_semaphore()
+
+        def signal(pr, pc):
+            pl.semaphore_signal(sem, inc=1, device_id={"pr": pr, "pc": pc}, device_id_type=MESH)
+
+        for n in range(1, 4):
+            signal((self.pr + n) % 4, self.pc)
+            signal(self.pr, self.place((self.y + n) % 4, self.z, self.c))
+            signal(self.pr, self.place(self.y, (self.z + n) % 4, self.c))
+        signal(self.pr, self.place(self.y, self.z, 1 - self.c))
+        roots = [(self.pr == p) & (self.pc == q) for p, q in ROOTS]
+        for p, q in ROOTS:
+
+            @pl.when((self.pr == p) & (self.pc != q))
+            def _():
+                signal(p, q)
+
+        is_root = roots[0] | roots[1] | roots[2]
+
+        @pl.when(is_root)
+        def _():
+            pl.semaphore_wait(sem, 41)
+
+        @pl.when(jnp.logical_not(is_root))
+        def _():
+            pl.semaphore_wait(sem, 10)
+
+    def slab(self, x, d):
+        return self.sbuf.at[x, d // 8, (d // 2) % 4, d % 2]
+
+    def scatter_copy(self, x, d):
+        src = self.a.at[pl.ds(pl.multiple_of(d * 64, 64), 64)]
+        return self.copy(src, self.slab(x, d), self.scat_s.at[d], self.scat_r.at[x], ROOTS[x][0], d)
+
+    def own_copy(self, x):
+        d = ROOTS[x][1]
+        return pltpu.make_async_copy(self.a.at[pl.ds(d * 64, 64)], self.slab(x, d), self.local.at[0])
+
+    def each_other(self, x, act):
+        p, q = ROOTS[x]
+
+        @pl.when((self.pr == p) & (self.pc == q))
+        def _():
+            @pl.loop(0, 32)
+            def _(d):
+                @pl.when(d != q)
+                def _():
+                    act(self.scatter_copy(x, d))
+
+    def scatter_start(self, x):
+        p, q = ROOTS[x]
+        self.each_other(x, lambda copy: copy.start())
+
+        @pl.when((self.pr == p) & (self.pc == q))
+        def _():
+            self.own_copy(x).start()
+
+    def x_copy(self, x, n):
+        mine = self.slab(x, self.pc)
+        return self.copy(mine, mine, self.x_s.at[x, n - 1], self.x_r.at[x], (self.pr + n) % 4, self.pc)
+
+    def spread_start(self, x):
+        p, q = ROOTS[x]
+
+        @pl.when((self.pr == p) & (self.pc == q))
+        def _():
+            self.own_copy(x).wait()
+
+        @pl.when((self.pr == p) & (self.pc != q))
+        def _():
+            self.scatter_copy(x, self.pc).wait_recv()
+
+        @pl.when(self.pr == p)
+        def _():
+            for n in range(1, 4):
+                self.x_copy(x, n).start()
+
+    def spread_wait(self, x):
+        @pl.when(self.pr != ROOTS[x][0])
+        def _():
+            self.x_copy(x, 1).wait_recv()
+
+    def gather_copies(self, x, phase, arriving=False):
+        y, z, c = self.y, self.z, self.c
+        if phase == 2:
+            oc = 1 - c
+            ref = self.sbuf.at[x, :, :, oc if arriving else c]
+            return [self.copy(ref, ref, self.ag_s.at[x, 12], self.ag_r.at[x, 12], self.pr, self.place(y, z, oc))]
+        out = []
+        for n in range(1, 4):
+            m = (4 - n) % 4 if arriving else 0
+            ym, zm = (y + m) % 4, (z + m) % 4
+            if phase == 0:
+                first = self.sbuf.at[x, ym, z, c, pl.ds(0, 32)]
+                second = self.sbuf.at[x, y, zm, c, pl.ds(32, 32)]
+                to_first, to_second = self.place((y + n) % 4, z, c), self.place(y, (z + n) % 4, c)
+            else:
+                first = self.sbuf.at[x, :, zm, c, pl.ds(0, 32)]
+                second = self.sbuf.at[x, ym, :, c, pl.ds(32, 32)]
+                to_first, to_second = self.place(y, (z + n) % 4, c), self.place((y + n) % 4, z, c)
+            k = phase * 6 + (n - 1) * 2
+            out.append(self.copy(first, first, self.ag_s.at[x, k], self.ag_r.at[x, k], self.pr, to_first))
+            out.append(self.copy(second, second, self.ag_s.at[x, k + 1], self.ag_r.at[x, k + 1], self.pr, to_second))
+        return out
+
+    def gather_start(self, x, phase):
+        for copy in self.gather_copies(x, phase):
+            copy.start()
+
+    def gather_wait(self, x, phase):
+        for copy in self.gather_copies(x, phase, arriving=True):
+            copy.wait_recv()
+
+    def b_copy(self, k, n):
+        return self.copy(
+            self.a.at[pl.ds(0, 4 * NB)], self.bbuf.at[k], self.b_s.at[n - 1], self.b_r.at[k], (self.pr + n) % 4, self.pc
+        )
+
+    def b_own(self, k):
+        return pltpu.make_async_copy(self.a.at[pl.ds(0, 4 * NB)], self.bbuf.at[k], self.local.at[1])
+
+    def b_start(self):
+        for k in range(2):
+
+            @pl.when(self.pr == k)
+            def _():
+                self.b_own(k).start()
+                for n in range(1, 4):
+                    self.b_copy(k, n).start()
+
+    def b_wait(self):
+        for k in range(2):
+
+            @pl.when(self.pr == k)
+            def _():
+                self.b_own(k).wait()
+
+            @pl.when(self.pr != k)
+            def _():
+                self.b_copy(k, 1).wait_recv()
+
+    def finish(self):
+        for x in range(3):
+            self.each_other(x, lambda copy: copy.wait_send())
+
+            @pl.when(self.pr == ROOTS[x][0])
+            def _():
+                for n in range(1, 4):
+                    self.x_copy(x, n).wait_send()
+
+            for phase in range(3):
+                for copy in self.gather_copies(x, phase):
+                    copy.wait_send()
+        for k in range(2):
+
+            @pl.when(self.pr == k)
+            def _():
+                for n in range(1, 4):
+                    self.b_copy(k, n).wait_send()
+
+
+def spread_rows(ref):
+    return [ref[pl.ds(c, NB, stride=4), :] for c in range(4)]
+
+
+def factor_kernel(a_ref, top_ref, q_ref, sbuf, bbuf, m, u, g, r, x, w, *sems):
+    net = Links(a_ref, sbuf, bbuf, *sems)
+    pr, pc = net.pr, net.pc
+    flat = sbuf.reshape(3, 4 * NB, T)
+    net.barrier()
+    net.scatter_start(0)
+    net.spread_start(0)
+    net.scatter_start(1)
+    net.scatter_start(2)
+    net.spread_wait(0)
+    net.gather_start(0, 0)
+    net.gather_wait(0, 0)
+    net.gather_start(0, 1)
+    net.spread_start(1)
+    net.spread_start(2)
+    net.gather_wait(0, 1)
+    net.gather_start(0, 2)
+    net.gather_wait(0, 2)
+    for c, piece in enumerate(spread_rows(flat.at[0])):
+        m[0:NB, c * T : (c + 1) * T] = piece
+
+    def after(t):
+        if t == 0:
+            for i in (1, 2):
+                net.spread_wait(i)
+                net.gather_start(i, 0)
+            net.b_start()
+        elif t < 3:
+            for i in (1, 2):
+                net.gather_wait(i, t - 1)
+                net.gather_start(i, t)
+
+    def solve_second():
+        for i in (1, 2):
+            net.gather_wait(i, 2)
+        net.b_wait()
+        for c, piece in enumerate(spread_rows(flat.at[1])):
+            r[:, c * T : (c + 1) * T] = piece
+        for c, piece in enumerate(spread_rows(bbuf.at[0])):
+            r[:, NB + c * T : NB + (c + 1) * T] = piece
+        for t in range(4):
+            a, b = t * T, (t + 1) * T
+            acc = r[a:b, :]
+            if t:
+                acc = acc - dot(u[0:a, a:b], x[0:a, :], 0, 0)
+            x[a:b, :] = dot(g[a:b, :], acc)
+        r[...] = dot(x[:, 0:NB], x[...], 0, 0)
+        for c, piece in enumerate(spread_rows(flat.at[2])):
+            m[NB:, c * T : (c + 1) * T] = piece - r[:, c * T : (c + 1) * T]
+        for c, piece in enumerate(spread_rows(bbuf.at[1])):
+            w[NB:, c * T : (c + 1) * T] = piece - r[:, NB + c * T : NB + (c + 1) * T]
 
     @pl.loop(0, NT)
     def _(t):
         o = pl.multiple_of(t * T, T)
-        rows = [m[pl.ds(o + 8 * i, 8), pl.ds(o, T)] for i in range(T // 8)]
+        oc = pl.multiple_of((t % 4) * T, T)
+        rows = [m[pl.ds(o + 8 * i, 8), pl.ds(oc, T)] for i in range(T // 8)]
         inv_rows, fac_rows = factor_tile(rows)
         for i in range(T // 8):
-            g_ref[pl.ds(o + 8 * i, 8), :] = inv_rows[i]
-            u_ref[pl.ds(o + 8 * i, 8), pl.ds(o, T)] = fac_rows[i]
+            g[pl.ds(o + 8 * i, 8), :] = inv_rows[i]
+            u[pl.ds(o + 8 * i, 8), pl.ds(oc, T)] = fac_rows[i]
         for ts in range(NT - 1):
 
             @pl.when(t == ts)
             def _():
-                a, b = ts * T, (ts + 1) * T
-                u = dot(g_ref[a:b, :], m[a:b, b:])
-                u_ref[a:b, b:] = u
-                for i in range(ts + 1, NT):
-                    lo = (i - ts - 1) * T
-                    m[i * T : (i + 1) * T, i * T :] -= dot(u[:, lo : lo + T], u[:, lo:], 0, 0)
-
-    for t in range(NT):
+                if ts == 3:
+                    solve_second()
+                    return
+                base = ts // 4 * NB
+                a, b = ts % 4 * T, (ts % 4 + 1) * T
+                piece = dot(g[base + a : base + b, :], m[base + a : base + b, b:])
+                u[base + a : base + b, b:] = piece
+                for i in range(ts % 4 + 1, 4):
+                    lo = i * T - b
+                    m[base + i * T : base + (i + 1) * T, i * T :] -= dot(piece[:, lo : lo + T], piece[:, lo:], 0, 0)
+                after(ts)
+
+    w[0:NB, :] = x[:, NB:]
+    for t in range(4):
         a, b = t * T, (t + 1) * T
-        acc = b_ref[a:b, :]
+        acc = w[NB + a : NB + b, :]
         if t:
-            acc = acc - dot(u_ref[0:a, a:b], w_ref[0:a, :], 0, 0)
-        w_ref[a:b, :] = dot(g_ref[a:b, :], acc)
-
-    top_ref[...] = w_ref[pl.ds(pl.multiple_of(jnp.minimum(pr, 1) * NB, NB), NB), :]
+            acc = acc - dot(u[NB : NB + a, a:b], w[NB : NB + a, :], 0, 0)
+        w[NB + a : NB + b, :] = dot(g[NB + a : NB + b, :], acc)
+
+    top_ref[...] = w[pl.ds(pl.multiple_of(jnp.minimum(pr, 1) * NB, NB), NB), :]
     for k in range(2):
 
         @pl.when((pc == k) & (pr == k))
         def _():
             for i in range(NB // T):
                 for j in range(NB // T):
-                    a, b = k * NB + i * T, k * NB + j * T
                     if j <= i:
-                        piece = u_ref[b : b + T, a : a + T].T
+                        piece = u[k * NB + j * T : k * NB + (j + 1) * T, i * T : (i + 1) * T].T
                     else:
                         piece = jnp.zeros((T, T), jnp.float32)
                     top_ref[i * T : (i + 1) * T, j * T : (j + 1) * T] = piece
@@ -119,32 +354,51 @@
     def _():
         row = lax.broadcasted_iota(jnp.int32, (N2, NB), 0)
         col = lax.broadcasted_iota(jnp.int32, (N2, NB), 1)
-        w_ref[...] = jnp.where(row == col + pc * NB, -1.0, 0.0)
-
-    for t in reversed(range(NT)):
-        a, b = t * T, (t + 1) * T
-        acc = w_ref[a:b, :]
-        if t < NT - 1:
-            acc = acc - dot(u_ref[a:b, b:], q_ref[b:, :])
-        q_ref[a:b, :] = dot(g_ref[a:b, :], acc, 0, 0)
-
-
-def factor(s, b):
+        w[...] = jnp.where(row == col + pc * NB, -1.0, 0.0)
+
+    for half in (NB, 0):
+        if half == 0:
+            w[0:NB, :] = w[0:NB, :] - dot(x[:, 0:NB], q_ref[NB:, :])
+        for t in reversed(range(4)):
+            a, b = t * T, (t + 1) * T
+            acc = w[half + a : half + b, :]
+            if t < 3:
+                acc = acc - dot(u[half + a : half + b, b:], q_ref[half + b : half + NB, :])
+            q_ref[half + a : half + b, :] = dot(g[half + a : half + b, :], acc, 0, 0)
+    net.finish()
+
+
+def factor(a):
     vmem = pl.BlockSpec(memory_space=pltpu.VMEM)
+    f32 = jnp.float32
+    dma = pltpu.SemaphoreType.DMA
     return pl.pallas_call(
         factor_kernel,
-        out_shape=(jax.ShapeDtypeStruct((NB, NB), jnp.float32), jax.ShapeDtypeStruct((N2, NB), jnp.float32)),
-        in_specs=[vmem, vmem],
+        out_shape=(jax.ShapeDtypeStruct((NB, NB), f32), jax.ShapeDtypeStruct((N2, NB), f32)),
+        in_specs=[pl.BlockSpec(memory_space=pl.ANY)],
         out_specs=(vmem, vmem),
         scratch_shapes=[
-            pltpu.VMEM((N2, N2), jnp.float32),
-            pltpu.VMEM((N2, N2), jnp.float32),
-            pltpu.VMEM((N2, T), jnp.float32),
-            pltpu.VMEM((N2, NB), jnp.float32),
+            pltpu.VMEM((3, 4, 4, 2, 64, T), f32),
+            pltpu.VMEM((2, 4 * NB, T), f32),
+            pltpu.VMEM((N2, NB), f32),
+            pltpu.VMEM((N2, NB), f32),
+            pltpu.VMEM((N2, T), f32),
+            pltpu.VMEM((NB, N2), f32),
+            pltpu.VMEM((NB, N2), f32),
+            pltpu.VMEM((N2, NB), f32),
+            dma((2,)),
+            dma((32,)),
+            dma((3,)),
+            dma((3, 3)),
+            dma((3,)),
+            dma((3, 13)),
+            dma((3, 13)),
+            dma((3,)),
+            dma((2,)),
         ],
-        compiler_params=pltpu.CompilerParams(vmem_limit_bytes=48 << 20),
-        cost_estimate=pl.CostEstimate(flops=40_000_000_000, bytes_accessed=10_000_000, transcendentals=0),
-    )(s, b)
+        compiler_params=pltpu.CompilerParams(vmem_limit_bytes=48 << 20, collective_id=0, has_side_effects=True),
+        cost_estimate=pl.CostEstimate(flops=60_000_000_000, bytes_accessed=10_000_000, transcendentals=0),
+    )(a)
 
 
 def split(x):
@@ -203,11 +457,6 @@
 def body(matrix):
     flat = matrix.reshape(8 * NB * 4, T)
     first = matrix[0, 0].reshape(NB, NB)
-    pr = lax.axis_index("pr")
-    pc = lax.axis_index("pc")
-    owner = [(pr == 0) & (pc == 0), (pr == 0) & (pc == 1), (pr == 1) & (pc == 1)]
-    s = lax.psum(jnp.stack([jnp.where(o, first, 0.0) for o in owner]), ("pr", "pc"))
-    b = lax.all_gather(first, "pr")[:2].reshape(N2, NB)
     turned = first.T
     mine = []
     for k in range(2):
@@ -218,7 +467,7 @@
             got = one if got is None else got + one
         mine.append(got)
     panel = lax.all_gather(jnp.stack(mine), "pc")
-    top, q = factor(s, b)
+    top, q = factor(flat)
     return update(flat, panel, q, top).reshape(matrix.shape)
 
 

time: 328 us -> 202 us (0.62)
  the two profiles are of different devices: /device:TPU:7 before, /device:TPU:1 now
where the time goes in v2:
time: 202 us; the launch traced here: 201 us
  Pallas kernels  151 us (75%)
  starting transfers between devices  27.4 us (14%)
  between operations  13.5 us (7%)
  waiting for transfers between devices  4.69 us (2%)
  local copies, waits for them, and re-layouts  3.32 us (2%)
    pallas_call x1, Pallas kernels, factor(): pl.pallas_call(factor_kernel, out_shape=(jax.ShapeDtypeStruct((NB, NB), f...  132 us
    ppermute x8, starting transfers between devices, body(): one = lax.ppermute(turned[part * T:(part + 1) * T], ('pr', 'pc'), pairs)  27.4 us
    pallas_call x1, Pallas kernels, update(): pl.pallas_call(update_kernel, grid=(8,), out_shape=jax.ShapeDtypeStruct(a...  19.5 us
    ppermute x8, waiting for transfers between devices, body(): one = lax.ppermute(turned[part * T:(part + 1) * T], ('pr', 'pc'), pairs)  4.65 us
  transfers between devices with their start and end apart: 9, of which 2 were waited for; matrix products, arithmetic and copies ran while one was open for 0% of the time, Pallas kernels for 66%

profile of v2, /device:TPU:1, one launch (start us, length us, event | category | flops | bytes accessed | tf_op | source)
XLA Modules:
  0.0 201.5 jit_solution(5176845370144947704)
XLA Ops:
  6.5 0.0 all-gather.3.cloned.1.call-start
  6.5 1.9 slice.19
  8.5 1.3 copy.6
  9.8 0.1 fusion
  9.9 1.3 collective-permute-start.5
  11.2 0.7 collective-permute-start.7
  11.9 0.7 collective-permute-start.6
  12.6 0.7 collective-permute-start.4
  13.2 10.1 %collective-permute-start.1 = (f32[128,512]{1,0:T(8,128)S(1)}, f32[128,512]{1,0:T(8,128)S(1)}, u32[]{:S(2)}, u32[]{:S(2)}) collective-permute-start(f32[128,512]{1,0:T(8,128)S(1)} %get-tuple-element.9), channel_id=1, source_target_pairs={{0,1},{1,33},{2,65},{3,97},{4,5},{5,37},{6,69},{7,101},{8,9},{9,41... | collective-permute-start | bytes 786440 | tf_op jit(solution)/shard_map/ppermute | solution.py:466
  23.3 0.0 collective-permute-done.5
  23.4 1.3 collective-permute-start.3
  24.7 0.0 collective-permute-done.7
  24.7 11.4 %collective-permute-start.2 = (f32[128,512]{1,0:T(8,128)S(1)}, f32[128,512]{1,0:T(8,128)S(1)}, u32[]{:S(2)}, u32[]{:S(2)}) collective-permute-start(f32[128,512]{1,0:T(8,128)S(1)} %get-tuple-element.11), channel_id=1, source_target_pairs={{0,2},{1,34},{2,66},{3,98},{4,6},{5,38},{6,70},{7,102},{8,10},{9,4... | collective-permute-start | bytes 786440 | tf_op jit(solution)/shard_map/ppermute | solution.py:466
  36.1 0.0 collective-permute-done.6
  36.1 1.3 collective-permute-start
  37.4 0.0 collective-permute-done.4
  37.4 0.1 add_bitcast_fusion
  37.5 0.0 collective-permute-done.1
  37.5 0.0 collective-permute-done.3
  37.5 1.8 collective-permute-done.2
  39.3 2.8 %collective-permute-done = f32[128,512]{1,0:T(8,128)S(1)} collective-permute-done((f32[128,512]{1,0:T(8,128)S(1)}, f32[128,512]{1,0:T(8,128)S(1)}, u32[]{:S(2)}, u32[]{:S(2)}) %collective-permute-start) | collective-permute-done | bytes 262176 | tf_op jit(solution)/shard_map/ppermute | solution.py:466
  42.1 0.1 add_bitcast_fusion.1
  42.2 0.8 pad_maximum_fusion
  43.1 0.0 all-gather.3.cloned.1.call-update
  43.1 132.0 %shard_map.17 = (f32[512,512]{1,0:T(8,128)S(1)}, f32[1024,512]{1,0:T(8,128)S(1)}) custom-call(f32[16384,128]{1,0:T(8,128)} %bitcast.11), custom_call_target="tpu_custom_call" | custom-call | flops 60000002048 | bytes 10000000 | tf_op jit(solution)/shard_map/pallas_call | solution.py:375
  175.1 0.0 all-gather.3.cloned.1.call-done
  175.2 19.5 %shard_map.18 = f32[16384,128]{1,0:T(8,128)} custom-call(f32[16384,128]{1,0:T(8,128)} %bitcast.12, f32[32,2,128,512]{3,2,1,0:T(8,128)} %bitcast.13, f32[1024,512]{1,0:T(8,128)S(1)} %get-tuple-element.7.q_ref, f32[512,512]{1,0:T(8,128)S(1)} %get-tuple-element.8.top_ref), custom_call_target="tpu_custom_call" | custom-call | flops 12999999488 | bytes 34000000 | tf_op jit(solution)/shard_map/pallas_call | solution.py:440
Async XLA Ops:
  6.5 168.6 %all-gather.3.cloned.1.call-start = ((), (), s32[]{:S(2)}) async-start(), calls=%async_computation | async-start | bytes 17301504 | tf_op jit(solution)/shard_map/all_gather | solution.py:469
  9.9 13.5 %collective-permute-start.5 = (f32[128,512]{1,0:T(8,128)S(1)}, f32[128,512]{1,0:T(8,128)S(1)}, u32[]{:S(2)}, u32[]{:S(2)}) collective-permute-start(f32[128,512]{1,0:T(8,128)S(1)} %get-tuple-element.9), channel_id=1, source_target_pairs={{32,1},{33,33},{34,65},{35,97},{36,5},{37,37},{38,69},{39,101},{40... | collective-permute-start | bytes 786440 | tf_op jit(solution)/shard_map/ppermute | solution.py:466
  11.2 13.5 %collective-permute-start.7 = (f32[128,512]{1,0:T(8,128)S(1)}, f32[128,512]{1,0:T(8,128)S(1)}, u32[]{:S(2)}, u32[]{:S(2)}) collective-permute-start(f32[128,512]{1,0:T(8,128)S(1)} %get-tuple-element.10), channel_id=1, source_target_pairs={{32,3},{33,35},{34,67},{35,99},{36,7},{37,39},{38,71},{39,103},{40... | collective-permute-start | bytes 786440 | tf_op jit(solution)/shard_map/ppermute | solution.py:466
  11.9 24.2 %collective-permute-start.6 = (f32[128,512]{1,0:T(8,128)S(1)}, f32[128,512]{1,0:T(8,128)S(1)}, u32[]{:S(2)}, u32[]{:S(2)}) collective-permute-start(f32[128,512]{1,0:T(8,128)S(1)} %get-tuple-element.11), channel_id=1, source_target_pairs={{32,2},{33,34},{34,66},{35,98},{36,6},{37,38},{38,70},{39,102},{40... | collective-permute-start | bytes 786440 | tf_op jit(solution)/shard_map/ppermute | solution.py:466
  12.6 24.8 %collective-permute-start.4 = (f32[128,512]{1,0:T(8,128)S(1)}, f32[128,512]{1,0:T(8,128)S(1)}, u32[]{:S(2)}, u32[]{:S(2)}) collective-permute-start(f32[128,512]{1,0:T(8,128)S(1)} %get-tuple-element.12), channel_id=1, source_target_pairs={{32,0},{33,32},{34,64},{35,96},{36,4},{37,36},{38,68},{39,100},{40... | collective-permute-start | bytes 786440 | tf_op jit(solution)/shard_map/ppermute | solution.py:466
  13.2 24.3 %collective-permute-start.1 = (f32[128,512]{1,0:T(8,128)S(1)}, f32[128,512]{1,0:T(8,128)S(1)}, u32[]{:S(2)}, u32[]{:S(2)}) collective-permute-start(f32[128,512]{1,0:T(8,128)S(1)} %get-tuple-element.9), channel_id=1, source_target_pairs={{0,1},{1,33},{2,65},{3,97},{4,5},{5,37},{6,69},{7,101},{8,9},{9,41... | collective-permute-start | bytes 786440 | tf_op jit(solution)/shard_map/ppermute | solution.py:466
  23.4 14.1 %collective-permute-start.3 = (f32[128,512]{1,0:T(8,128)S(1)}, f32[128,512]{1,0:T(8,128)S(1)}, u32[]{:S(2)}, u32[]{:S(2)}) collective-permute-start(f32[128,512]{1,0:T(8,128)S(1)} %get-tuple-element.10), channel_id=1, source_target_pairs={{0,3},{1,35},{2,67},{3,99},{4,7},{5,39},{6,71},{7,103},{8,11},{9,4... | collective-permute-start | bytes 786440 | tf_op jit(solution)/shard_map/ppermute | solution.py:466
  24.7 14.7 %collective-permute-start.2 = (f32[128,512]{1,0:T(8,128)S(1)}, f32[128,512]{1,0:T(8,128)S(1)}, u32[]{:S(2)}, u32[]{:S(2)}) collective-permute-start(f32[128,512]{1,0:T(8,128)S(1)} %get-tuple-element.11), channel_id=1, source_target_pairs={{0,2},{1,34},{2,66},{3,98},{4,6},{5,38},{6,70},{7,102},{8,10},{9,4... | collective-permute-start | bytes 786440 | tf_op jit(solution)/shard_map/ppermute | solution.py:466
  36.1 6.1 %collective-permute-start = (f32[128,512]{1,0:T(8,128)S(1)}, f32[128,512]{1,0:T(8,128)S(1)}, u32[]{:S(2)}, u32[]{:S(2)}) collective-permute-start(f32[128,512]{1,0:T(8,128)S(1)} %get-tuple-element.12), channel_id=1, source_target_pairs={{0,0},{1,32},{2,64},{3,96},{4,4},{5,36},{6,68},{7,100},{8,8},{9,40... | collective-permute-start | bytes 786440 | tf_op jit(solution)/shard_map/ppermute | solution.py:466
Sparse Core Ops, SparseCore 0:
  43.2 82.7 all-gather.2

commit v3 on v2

--- a/solution.py
+++ b/solution.py
@@ -71,12 +71,21 @@
 
 
 class Links:
-    def __init__(self, a, sbuf, bbuf, local, scat_s, scat_r, x_s, x_r, ag_s, ag_r, b_s, b_r):
+    def __init__(self, a, pan, sbuf, bbuf, tbuf, local, scat_s, scat_r, x_s, x_r, ag_s, ag_r, b_s, b_r, t_s, t_r, p_s, p_r, c_s, c_r):
         self.a, self.sbuf, self.bbuf, self.local = a, sbuf, bbuf, local
+        self.pan, self.tbuf, self.t_s, self.t_r = pan, tbuf, t_s, t_r
+        self.p_s, self.p_r, self.c_s, self.c_r = p_s, p_r, c_s, c_r
         self.scat_s, self.scat_r, self.x_s, self.x_r = scat_s, scat_r, x_s, x_r
         self.ag_s, self.ag_r, self.b_s, self.b_r = ag_s, ag_r, b_s, b_r
         self.pr, self.pc = lax.axis_index("pr"), lax.axis_index("pc")
         self.y, self.z, self.c = self.pc // 8, (self.pc // 2) % 4, self.pc % 2
+        self.row_owner = self.pr < 2
+        self.dst_pr = self.pc % 4
+        self.dst_z = 2 * (self.z // 2) + (self.pr + self.z) % 2
+        self.keeps = (self.pr == 0) & (self.dst_pr == 0)
+        self.src_pr = (self.z + self.pr // 2) % 2
+        self.src_pc = self.place(self.y, 2 * (self.z // 2) + self.pr // 2, self.pr % 2)
+        self.from_self = (self.src_pr == self.pr) & (self.src_pc == self.pc)
 
     def copy(self, src, dst, send, recv, pr, pc):
         return pltpu.make_async_remote_copy(
@@ -104,15 +113,20 @@
             def _():
                 signal(p, q)
 
+        @pl.when(jnp.logical_not(self.from_self))
+        def _():
+            signal(self.src_pr, self.src_pc)
+
         is_root = roots[0] | roots[1] | roots[2]
 
-        @pl.when(is_root)
-        def _():
-            pl.semaphore_wait(sem, 41)
-
-        @pl.when(jnp.logical_not(is_root))
-        def _():
-            pl.semaphore_wait(sem, 10)
+        sources = self.row_owner & jnp.logical_not(self.keeps)
+        other = jnp.logical_not(is_root)
+        for base, group in ((41, is_root), (10, other)):
+            for more, kind in ((2, sources), (1, self.keeps), (0, jnp.logical_not(self.row_owner))):
+
+                @pl.when(group & kind)
+                def _():
+                    pl.semaphore_wait(sem, base + more)
 
     def slab(self, x, d):
         return self.sbuf.at[x, d // 8, (d // 2) % 4, d % 2]
@@ -208,27 +222,139 @@
     def b_own(self, k):
         return pltpu.make_async_copy(self.a.at[pl.ds(0, 4 * NB)], self.bbuf.at[k], self.local.at[1])
 
+    def own_start(self):
+        for k in range(2):
+
+            @pl.when(self.pr == k)
+            def _():
+                self.b_own(k).start()
+
+    def turn(self):
+        for k in range(2):
+
+            @pl.when(self.pr == k)
+            def _():
+                self.b_own(k).wait()
+                for s in range(4):
+                    self.tbuf[s] = self.bbuf.at[k][pl.ds(s, NB, stride=4), :].T
+
+    def t_refs(self, s, core):
+        return self.tbuf.at[s, pl.ds(core * 64, 64)], self.pan.at[self.y, self.dst_z, s, core]
+
+    def t_copy(self, s, core):
+        src, dst = self.t_refs(s, core)
+        to = self.place(self.y, self.dst_z, core)
+        return self.copy(src, dst, self.t_s.at[s, core], self.t_r.at[s], self.dst_pr, to)
+
+    def t_local(self, s):
+        src, dst = self.t_refs(s, 0)
+        return pltpu.make_async_copy(src, dst, self.local.at[2 + s])
+
+    def t_start(self, s):
+        @pl.when(self.keeps)
+        def _():
+            self.t_local(s).start()
+
+        @pl.when(self.row_owner & jnp.logical_not(self.keeps))
+        def _():
+            self.t_copy(s, 0).start()
+
+        @pl.when(self.row_owner)
+        def _():
+            self.t_copy(s, 1).start()
+
+    def t_wait(self, s):
+        @pl.when(self.from_self)
+        def _():
+            self.t_local(s).wait()
+
+        @pl.when(jnp.logical_not(self.from_self))
+        def _():
+            mine = self.pan.at[self.y, self.z, s, self.c]
+            self.copy(mine, mine, self.t_s.at[s, 0], self.t_r.at[s], self.src_pr, self.src_pc).wait_recv()
+
+    def ring_part(self, s, order, phase, v, half):
+        first, rows = (0, 32) if half is None else (16 * half, 16)
+        at = pl.ds(32 * order + first, rows)
+        along_y = (order + phase) % 2 == 0
+        if phase == 0:
+            return self.pan.at[v, self.z, s, self.c, at] if along_y else self.pan.at[self.y, v, s, self.c, at]
+        return self.pan.at[v, :, s, self.c, at] if along_y else self.pan.at[:, v, s, self.c, at]
+
+    def ring_copies(self, s, phase, step, arriving=False):
+        out = []
+        for order in range(2):
+            along_y = (order + phase) % 2 == 0
+            me = self.y if along_y else self.z
+            for way in range(2):
+                n = 1 if way == 0 else 3
+                to = (me + n) % 4
+                dev = self.place(to, self.z, self.c) if along_y else self.place(self.y, to, self.c)
+                back = (step + 1 if arriving else step) * (4 - n)
+                ref = self.ring_part(s, order, phase, (me + back) % 4, None if step == 0 else way)
+                k = ((order * 2 + phase) * 2 + step) * 2 + way
+                out.append(self.copy(ref, ref, self.p_s.at[s, k], self.p_r.at[s, k], self.pr, dev))
+        return out
+
+    def core_copy(self, s, arriving=False):
+        oc = 1 - self.c
+        ref = self.pan.at[:, :, s, oc if arriving else self.c]
+        return self.copy(ref, ref, self.c_s.at[s], self.c_r.at[s], self.pr, self.place(self.y, self.z, oc))
+
+    def panel_stage(self, s, stage):
+        if stage == 0:
+            self.t_start(s)
+            return
+        if stage == 1:
+            self.t_wait(s)
+        elif stage < 6:
+            for copy in self.ring_copies(s, (stage - 2) // 2, (stage - 2) % 2, arriving=True):
+                copy.wait_recv()
+        else:
+            self.core_copy(s, arriving=True).wait_recv()
+            return
+        if stage < 5:
+            for copy in self.ring_copies(s, (stage - 1) // 2, (stage - 1) % 2):
+                copy.start()
+        else:
+            self.core_copy(s).start()
+
+    def panel_slot(self, slot):
+        for s in range(4):
+            if 0 <= slot - s <= 6:
+                self.panel_stage(s, slot - s)
+
     def b_start(self):
         for k in range(2):
 
             @pl.when(self.pr == k)
             def _():
-                self.b_own(k).start()
                 for n in range(1, 4):
                     self.b_copy(k, n).start()
 
     def b_wait(self):
         for k in range(2):
 
-            @pl.when(self.pr == k)
-            def _():
-                self.b_own(k).wait()
-
             @pl.when(self.pr != k)
             def _():
                 self.b_copy(k, 1).wait_recv()
 
     def finish(self):
+        for s in range(4):
+
+            @pl.when(self.row_owner & jnp.logical_not(self.keeps))
+            def _():
+                self.t_copy(s, 0).wait_send()
+
+            @pl.when(self.row_owner)
+            def _():
+                self.t_copy(s, 1).wait_send()
+
+            for phase in range(2):
+                for step in range(2):
+                    for copy in self.ring_copies(s, phase, step):
+                        copy.wait_send()
+            self.core_copy(s).wait_send()
         for x in range(3):
             self.each_other(x, lambda copy: copy.wait_send())
 
@@ -252,12 +378,14 @@
     return [ref[pl.ds(c, NB, stride=4), :] for c in range(4)]
 
 
-def factor_kernel(a_ref, top_ref, q_ref, sbuf, bbuf, m, u, g, r, x, w, *sems):
-    net = Links(a_ref, sbuf, bbuf, *sems)
+def factor_kernel(a_ref, top_ref, q_ref, pan, sbuf, bbuf, tbuf, m, u, g, r, x, w, *sems):
+    net = Links(a_ref, pan, sbuf, bbuf, tbuf, *sems)
     pr, pc = net.pr, net.pc
     flat = sbuf.reshape(3, 4 * NB, T)
+    net.own_start()
     net.barrier()
     net.scatter_start(0)
+    net.turn()
     net.spread_start(0)
     net.scatter_start(1)
     net.scatter_start(2)
@@ -269,6 +397,7 @@
     net.spread_start(2)
     net.gather_wait(0, 1)
     net.gather_start(0, 2)
+    net.panel_slot(0)
     net.gather_wait(0, 2)
     for c, piece in enumerate(spread_rows(flat.at[0])):
         m[0:NB, c * T : (c + 1) * T] = piece
@@ -278,31 +407,31 @@
             for i in (1, 2):
                 net.spread_wait(i)
                 net.gather_start(i, 0)
-            net.b_start()
         elif t < 3:
             for i in (1, 2):
                 net.gather_wait(i, t - 1)
                 net.gather_start(i, t)
+        net.panel_slot(t + 1)
+        if t == 2:
+            net.b_start()
+
+    def forward(lo, dst, rhs):
+        for t in range(4):
+            a, b = t * T, (t + 1) * T
+            acc = rhs[a:b, :]
+            if t:
+                acc = acc - dot(u[lo : lo + a, a:b], dst[0:a, :], 0, 0)
+            dst[a:b, :] = dot(g[lo + a : lo + b, :], acc)
 
     def solve_second():
         for i in (1, 2):
             net.gather_wait(i, 2)
-        net.b_wait()
         for c, piece in enumerate(spread_rows(flat.at[1])):
             r[:, c * T : (c + 1) * T] = piece
-        for c, piece in enumerate(spread_rows(bbuf.at[0])):
-            r[:, NB + c * T : NB + (c + 1) * T] = piece
-        for t in range(4):
-            a, b = t * T, (t + 1) * T
-            acc = r[a:b, :]
-            if t:
-                acc = acc - dot(u[0:a, a:b], x[0:a, :], 0, 0)
-            x[a:b, :] = dot(g[a:b, :], acc)
-        r[...] = dot(x[:, 0:NB], x[...], 0, 0)
+        forward(0, x, r)
+        r[...] = dot(x[...], x[...], 0, 0)
         for c, piece in enumerate(spread_rows(flat.at[2])):
             m[NB:, c * T : (c + 1) * T] = piece - r[:, c * T : (c + 1) * T]
-        for c, piece in enumerate(spread_rows(bbuf.at[1])):
-            w[NB:, c * T : (c + 1) * T] = piece - r[:, NB + c * T : NB + (c + 1) * T]
 
     @pl.loop(0, NT)
     def _(t):
@@ -313,12 +442,14 @@
         for i in range(T // 8):
             g[pl.ds(o + 8 * i, 8), :] = inv_rows[i]
             u[pl.ds(o + 8 * i, 8), pl.ds(oc, T)] = fac_rows[i]
-        for ts in range(NT - 1):
+        for ts in range(NT):
 
             @pl.when(t == ts)
             def _():
-                if ts == 3:
-                    solve_second()
+                if ts % 4 == 3:
+                    if ts == 3:
+                        solve_second()
+                    after(ts)
                     return
                 base = ts // 4 * NB
                 a, b = ts % 4 * T, (ts % 4 + 1) * T
@@ -329,13 +460,14 @@
                     m[base + i * T : base + (i + 1) * T, i * T :] -= dot(piece[:, lo : lo + T], piece[:, lo:], 0, 0)
                 after(ts)
 
-    w[0:NB, :] = x[:, NB:]
-    for t in range(4):
-        a, b = t * T, (t + 1) * T
-        acc = w[NB + a : NB + b, :]
-        if t:
-            acc = acc - dot(u[NB : NB + a, a:b], w[NB : NB + a, :], 0, 0)
-        w[NB + a : NB + b, :] = dot(g[NB + a : NB + b, :], acc)
+    net.b_wait()
+    for c, piece in enumerate(spread_rows(bbuf.at[0])):
+        r[:, c * T : (c + 1) * T] = piece
+    forward(0, w.at[0:NB], r)
+    r[...] = dot(x[...], w[0:NB, :], 0, 0)
+    for c, piece in enumerate(spread_rows(bbuf.at[1])):
+        r[:, c * T : (c + 1) * T] = piece - r[:, c * T : (c + 1) * T]
+    forward(NB, w.at[NB:N2], r)
 
     top_ref[...] = w[pl.ds(pl.multiple_of(jnp.minimum(pr, 1) * NB, NB), NB), :]
     for k in range(2):
@@ -358,13 +490,14 @@
 
     for half in (NB, 0):
         if half == 0:
-            w[0:NB, :] = w[0:NB, :] - dot(x[:, 0:NB], q_ref[NB:, :])
+            w[0:NB, :] = w[0:NB, :] - dot(x[...], q_ref[NB:, :])
         for t in reversed(range(4)):
             a, b = t * T, (t + 1) * T
             acc = w[half + a : half + b, :]
             if t < 3:
                 acc = acc - dot(u[half + a : half + b, b:], q_ref[half + b : half + NB, :])
             q_ref[half + a : half + b, :] = dot(g[half + a : half + b, :], acc, 0, 0)
+    net.panel_slot(9)
     net.finish()
 
 
@@ -374,19 +507,24 @@
     dma = pltpu.SemaphoreType.DMA
     return pl.pallas_call(
         factor_kernel,
-        out_shape=(jax.ShapeDtypeStruct((NB, NB), f32), jax.ShapeDtypeStruct((N2, NB), f32)),
+        out_shape=(
+            jax.ShapeDtypeStruct((NB, NB), f32),
+            jax.ShapeDtypeStruct((N2, NB), f32),
+            jax.ShapeDtypeStruct((4, 4, 4, 2, 64, NB), f32),
+        ),
         in_specs=[pl.BlockSpec(memory_space=pl.ANY)],
-        out_specs=(vmem, vmem),
+        out_specs=(vmem, vmem, pl.BlockSpec(memory_space=pl.ANY)),
         scratch_shapes=[
             pltpu.VMEM((3, 4, 4, 2, 64, T), f32),
             pltpu.VMEM((2, 4 * NB, T), f32),
+            pltpu.VMEM((4, T, NB), f32),
             pltpu.VMEM((N2, NB), f32),
             pltpu.VMEM((N2, NB), f32),
             pltpu.VMEM((N2, T), f32),
-            pltpu.VMEM((NB, N2), f32),
-            pltpu.VMEM((NB, N2), f32),
+            pltpu.VMEM((NB, NB), f32),
+            pltpu.VMEM((NB, NB), f32),
             pltpu.VMEM((N2, NB), f32),
-            dma((2,)),
+            dma((6,)),
             dma((32,)),
             dma((3,)),
             dma((3, 3)),
@@ -395,6 +533,12 @@
             dma((3, 13)),
             dma((3,)),
             dma((2,)),
+            dma((4, 2)),
+            dma((4,)),
+            dma((4, 16)),
+            dma((4, 16)),
+            dma((4,)),
+            dma((4,)),
         ],
         compiler_params=pltpu.CompilerParams(vmem_limit_bytes=48 << 20, collective_id=0, has_side_effects=True),
         cost_estimate=pl.CostEstimate(flops=60_000_000_000, bytes_accessed=10_000_000, transcendentals=0),
@@ -422,8 +566,9 @@
     keep = jnp.where(pc < 2, 0.0, 1.0)
     acc = None
     for k in range(2):
-        ph, plo = split(p_ref[:, k].reshape(NB, NB))
-        h, lo = qh[k * NB : (k + 1) * NB], ql[k * NB : (k + 1) * NB]
+        ph, plo = split(p_ref[0, k])
+        at = pl.ds(pl.multiple_of((k + pr // 2) % 2 * NB, NB), NB)
+        h, lo = qh[at, :], ql[at, :]
         part = mm(ph, h) + (mm(ph, lo) + mm(plo, h))
         acc = part if acc is None else acc + part
     for c in range(4):
@@ -443,7 +588,7 @@
         out_shape=jax.ShapeDtypeStruct(a.shape, jnp.float32),
         in_specs=[
             pl.BlockSpec((4 * NB, T), lambda l: (l, 0)),
-            pl.BlockSpec((4, 2, T, NB), lambda l: (l, 0, 0, 0)),
+            pl.BlockSpec((1, 2, NB, NB), lambda l: (l, 0, 0, 0)),
             pl.BlockSpec((N2, NB), lambda l: (0, 0)),
             pl.BlockSpec((NB, NB), lambda l: (0, 0)),
         ],
@@ -456,18 +601,8 @@
 
 def body(matrix):
     flat = matrix.reshape(8 * NB * 4, T)
-    first = matrix[0, 0].reshape(NB, NB)
-    turned = first.T
-    mine = []
-    for k in range(2):
-        got = None
-        for part in range(4):
-            pairs = [(k * 32 + i, (i % 4) * 32 + 4 * (i // 4) + part) for i in range(32)]
-            one = lax.ppermute(turned[part * T : (part + 1) * T], ("pr", "pc"), pairs)
-            got = one if got is None else got + one
-        mine.append(got)
-    panel = lax.all_gather(jnp.stack(mine), "pc")
-    top, q = factor(flat)
+    top, q, panel = factor(flat)
+    panel = panel.reshape(8, 2, NB, NB)
     return update(flat, panel, q, top).reshape(matrix.shape)
 
 

time: 202 us -> 153 us (0.76)
  the two profiles are of different devices: /device:TPU:1 before, /device:TPU:7 now
where the time goes in v3:
time: 153 us
  Pallas kernels  153 us (100%)
    pallas_call x1, Pallas kernels, factor(): pl.pallas_call(factor_kernel, out_shape=(jax.ShapeDtypeStruct((NB, NB), f...  133 us
    pallas_call x1, Pallas kernels, update(): pl.pallas_call(update_kernel, grid=(8,), out_shape=jax.ShapeDtypeStruct(a...  19.4 us

profile of v3, /device:TPU:7, one launch (start us, length us, event | category | flops | bytes accessed | tf_op | source)
XLA Modules:
  0.0 152.8 jit_solution(18049139672898689269)
XLA Ops:
  0.0 133.4 %shard_map.17 = (f32[512,512]{1,0:T(8,128)S(1)}, f32[1024,512]{1,0:T(8,128)S(1)}, f32[4,4,4,2,64,512]{5,4,3,2,1,0:T(8,128)}) custom-call(f32[16384,128]{1,0:T(8,128)} %bitcast.3), custom_call_target="tpu_custom_call" | custom-call | flops 60000002048 | bytes 10000000 | tf_op jit(solution)/shard_map/pallas_call | solution.py:508
  133.4 19.4 %shard_map.18 = f32[16384,128]{1,0:T(8,128)} custom-call(f32[16384,128]{1,0:T(8,128)} %bitcast.4, f32[8,2,512,512]{3,2,1,0:T(8,128)} %bitcast.5, f32[1024,512]{1,0:T(8,128)S(1)} %get-tuple-element.9.q_ref, f32[512,512]{1,0:T(8,128)S(1)} %get-tuple-element.10.top_ref), custom_call_target="tpu_custom_call" | custom-call | flops 12999999488 | bytes 34000000 | tf_op jit(solution)/shard_map/pallas_call | solution.py:585

commit v4 on v3

--- a/solution.py
+++ b/solution.py
@@ -71,21 +71,17 @@
 
 
 class Links:
-    def __init__(self, a, pan, sbuf, bbuf, tbuf, local, scat_s, scat_r, x_s, x_r, ag_s, ag_r, b_s, b_r, t_s, t_r, p_s, p_r, c_s, c_r):
-        self.a, self.sbuf, self.bbuf, self.local = a, sbuf, bbuf, local
-        self.pan, self.tbuf, self.t_s, self.t_r = pan, tbuf, t_s, t_r
+    def __init__(self, a, pan, sbuf, abuf, bt, local, scat_s, scat_r, x_s, x_r, ag_s, ag_r, b_s, b_r, f_s, t_s, t_r, p_s, p_r, c_s, c_r):
+        self.a, self.sbuf, self.abuf, self.bt, self.local = a, sbuf, abuf, bt, local
+        self.pan, self.f_s, self.t_s, self.t_r = pan, f_s, t_s, t_r
         self.p_s, self.p_r, self.c_s, self.c_r = p_s, p_r, c_s, c_r
         self.scat_s, self.scat_r, self.x_s, self.x_r = scat_s, scat_r, x_s, x_r
         self.ag_s, self.ag_r, self.b_s, self.b_r = ag_s, ag_r, b_s, b_r
         self.pr, self.pc = lax.axis_index("pr"), lax.axis_index("pc")
         self.y, self.z, self.c = self.pc // 8, (self.pc // 2) % 4, self.pc % 2
-        self.row_owner = self.pr < 2
-        self.dst_pr = self.pc % 4
-        self.dst_z = 2 * (self.z // 2) + (self.pr + self.z) % 2
-        self.keeps = (self.pr == 0) & (self.dst_pr == 0)
-        self.src_pr = (self.z + self.pr // 2) % 2
+        self.owner = self.pr == self.pc % 4
         self.src_pc = self.place(self.y, 2 * (self.z // 2) + self.pr // 2, self.pr % 2)
-        self.from_self = (self.src_pr == self.pr) & (self.src_pc == self.pc)
+        self.from_self = self.src_pc == self.pc
 
     def copy(self, src, dst, send, recv, pr, pc):
         return pltpu.make_async_remote_copy(
@@ -115,14 +111,12 @@
 
         @pl.when(jnp.logical_not(self.from_self))
         def _():
-            signal(self.src_pr, self.src_pc)
+            signal(self.pr, self.src_pc)
 
         is_root = roots[0] | roots[1] | roots[2]
 
-        sources = self.row_owner & jnp.logical_not(self.keeps)
-        other = jnp.logical_not(is_root)
-        for base, group in ((41, is_root), (10, other)):
-            for more, kind in ((2, sources), (1, self.keeps), (0, jnp.logical_not(self.row_owner))):
+        for base, group in ((41, is_root), (10, jnp.logical_not(is_root))):
+            for more, kind in ((3, self.owner), (0, jnp.logical_not(self.owner))):
 
                 @pl.when(group & kind)
                 def _():
@@ -214,54 +208,94 @@
         for copy in self.gather_copies(x, phase, arriving=True):
             copy.wait_recv()
 
-    def b_copy(self, k, n):
-        return self.copy(
-            self.a.at[pl.ds(0, 4 * NB)], self.bbuf.at[k], self.b_s.at[n - 1], self.b_r.at[k], (self.pr + n) % 4, self.pc
-        )
-
-    def b_own(self, k):
-        return pltpu.make_async_copy(self.a.at[pl.ds(0, 4 * NB)], self.bbuf.at[k], self.local.at[1])
+    def own_copy_in(self):
+        return pltpu.make_async_copy(self.a.at[pl.ds(0, 4 * NB)], self.abuf, self.local.at[1])
 
     def own_start(self):
-        for k in range(2):
-
-            @pl.when(self.pr == k)
-            def _():
-                self.b_own(k).start()
+        @pl.when(self.pr < 2)
+        def _():
+            self.own_copy_in().start()
 
     def turn(self):
         for k in range(2):
 
             @pl.when(self.pr == k)
             def _():
-                self.b_own(k).wait()
+                self.own_copy_in().wait()
                 for s in range(4):
-                    self.tbuf[s] = self.bbuf.at[k][pl.ds(s, NB, stride=4), :].T
-
-    def t_refs(self, s, core):
-        return self.tbuf.at[s, pl.ds(core * 64, 64)], self.pan.at[self.y, self.dst_z, s, core]
-
-    def t_copy(self, s, core):
-        src, dst = self.t_refs(s, core)
-        to = self.place(self.y, self.dst_z, core)
-        return self.copy(src, dst, self.t_s.at[s, core], self.t_r.at[s], self.dst_pr, to)
+                    self.bt[k, s] = self.abuf[pl.ds(s, NB, stride=4), :].T
+
+    def b_copy(self, k, s, way):
+        ref, n = self.bt.at[k, s], 3 if way else 1
+        return self.copy(ref, ref, self.b_s.at[s, way], self.b_r.at[k, s, 0], (self.pr + n) % 4, self.pc)
+
+    def f_copy(self, k, s, way):
+        ref, n = self.bt.at[k, s, pl.ds(64 * way, 64)], 3 if way else 1
+        return self.copy(ref, ref, self.f_s.at[k, s], self.b_r.at[k, s, way], (self.pr + n) % 4, self.pc)
+
+    def at_distance(self, k, n):
+        return self.pr == (k + n) % 4
+
+    def b_start(self, s):
+        for k in range(2):
+
+            @pl.when(self.at_distance(k, 0))
+            def _():
+                for way in range(2):
+                    self.b_copy(k, s, way).start()
+
+    def b_forward(self, s):
+        for k in range(2):
+            for way, n in ((0, 1), (1, 3)):
+
+                @pl.when(self.at_distance(k, n))
+                def _():
+                    self.b_copy(k, s, way).wait_recv()
+                    self.f_copy(k, s, way).start()
+
+    def b_wait(self, s):
+        for k in range(2):
+
+            @pl.when(self.at_distance(k, 2))
+            def _():
+                for way in range(2):
+                    self.f_copy(k, s, way).wait_recv()
+
+    def b_finish(self, s):
+        for k in range(2):
+
+            @pl.when(self.at_distance(k, 0))
+            def _():
+                for way in range(2):
+                    self.b_copy(k, s, way).wait_send()
+
+            for way, n in ((0, 1), (1, 3)):
+
+                @pl.when(self.at_distance(k, n))
+                def _():
+                    self.f_copy(k, s, way).wait_send()
+
+    def t_half(self, k, s, core):
+        z = self.z if k == 0 else 2 * (self.z // 2) + 1 - self.z % 2
+        return self.bt.at[k, s, pl.ds(core * 64, 64)], self.pan.at[self.y, z, s, core], z
 
     def t_local(self, s):
-        src, dst = self.t_refs(s, 0)
+        src, dst, _ = self.t_half(0, s, self.c)
         return pltpu.make_async_copy(src, dst, self.local.at[2 + s])
 
+    def t_copies(self, s):
+        out = []
+        for i, (k, core) in enumerate(((0, 1 - self.c), (1, 0), (1, 1))):
+            src, dst, z = self.t_half(k, s, core)
+            out.append(self.copy(src, dst, self.t_s.at[s, i], self.t_r.at[s], self.pr, self.place(self.y, z, core)))
+        return out
+
     def t_start(self, s):
-        @pl.when(self.keeps)
+        @pl.when(self.owner)
         def _():
             self.t_local(s).start()
-
-        @pl.when(self.row_owner & jnp.logical_not(self.keeps))
-        def _():
-            self.t_copy(s, 0).start()
-
-        @pl.when(self.row_owner)
-        def _():
-            self.t_copy(s, 1).start()
+            for copy in self.t_copies(s):
+                copy.start()
 
     def t_wait(self, s):
         @pl.when(self.from_self)
@@ -271,7 +305,7 @@
         @pl.when(jnp.logical_not(self.from_self))
         def _():
             mine = self.pan.at[self.y, self.z, s, self.c]
-            self.copy(mine, mine, self.t_s.at[s, 0], self.t_r.at[s], self.src_pr, self.src_pc).wait_recv()
+            self.copy(mine, mine, self.t_s.at[s, 0], self.t_r.at[s], self.pr, self.src_pc).wait_recv()
 
     def ring_part(self, s, order, phase, v, half):
         first, rows = (0, 32) if half is None else (16 * half, 16)
@@ -303,52 +337,39 @@
 
     def panel_stage(self, s, stage):
         if stage == 0:
+            self.b_start(s)
+        elif stage == 1:
+            self.b_forward(s)
+        elif stage == 2:
+            self.b_wait(s)
             self.t_start(s)
-            return
-        if stage == 1:
+        elif stage == 3:
             self.t_wait(s)
-        elif stage < 6:
-            for copy in self.ring_copies(s, (stage - 2) // 2, (stage - 2) % 2, arriving=True):
+        elif stage < 8:
+            for copy in self.ring_copies(s, (stage - 4) // 2, stage % 2, arriving=True):
                 copy.wait_recv()
         else:
             self.core_copy(s, arriving=True).wait_recv()
-            return
-        if stage < 5:
-            for copy in self.ring_copies(s, (stage - 1) // 2, (stage - 1) % 2):
+        if 3 <= stage < 7:
+            for copy in self.ring_copies(s, (stage - 3) // 2, (stage - 3) % 2):
                 copy.start()
-        else:
+        elif stage == 7:
             self.core_copy(s).start()
 
     def panel_slot(self, slot):
         for s in range(4):
-            if 0 <= slot - s <= 6:
+            if 0 <= slot - s <= 8:
                 self.panel_stage(s, slot - s)
-
-    def b_start(self):
-        for k in range(2):
-
-            @pl.when(self.pr == k)
-            def _():
-                for n in range(1, 4):
-                    self.b_copy(k, n).start()
-
-    def b_wait(self):
-        for k in range(2):
-
-            @pl.when(self.pr != k)
-            def _():
-                self.b_copy(k, 1).wait_recv()
 
     def finish(self):
         for s in range(4):
 
-            @pl.when(self.row_owner & jnp.logical_not(self.keeps))
-            def _():
-                self.t_copy(s, 0).wait_send()
-
-            @pl.when(self.row_owner)
-            def _():
-                self.t_copy(s, 1).wait_send()
+            self.b_finish(s)
+
+            @pl.when(self.owner)
+            def _():
+                for copy in self.t_copies(s):
+                    copy.wait_send()
 
             for phase in range(2):
                 for step in range(2):
@@ -366,26 +387,21 @@
             for phase in range(3):
                 for copy in self.gather_copies(x, phase):
                     copy.wait_send()
-        for k in range(2):
-
-            @pl.when(self.pr == k)
-            def _():
-                for n in range(1, 4):
-                    self.b_copy(k, n).wait_send()
 
 
 def spread_rows(ref):
     return [ref[pl.ds(c, NB, stride=4), :] for c in range(4)]
 
 
-def factor_kernel(a_ref, top_ref, q_ref, pan, sbuf, bbuf, tbuf, m, u, g, r, x, w, *sems):
-    net = Links(a_ref, pan, sbuf, bbuf, tbuf, *sems)
+def factor_kernel(a_ref, top_ref, q_ref, pan, sbuf, abuf, bt, m, u, g, r, x, w, *sems):
+    net = Links(a_ref, pan, sbuf, abuf, bt, *sems)
     pr, pc = net.pr, net.pc
     flat = sbuf.reshape(3, 4 * NB, T)
     net.own_start()
     net.barrier()
     net.scatter_start(0)
     net.turn()
+    net.panel_slot(0)
     net.spread_start(0)
     net.scatter_start(1)
     net.scatter_start(2)
@@ -397,7 +413,7 @@
     net.spread_start(2)
     net.gather_wait(0, 1)
     net.gather_start(0, 2)
-    net.panel_slot(0)
+    net.panel_slot(1)
     net.gather_wait(0, 2)
     for c, piece in enumerate(spread_rows(flat.at[0])):
         m[0:NB, c * T : (c + 1) * T] = piece
@@ -411,9 +427,7 @@
             for i in (1, 2):
                 net.gather_wait(i, t - 1)
                 net.gather_start(i, t)
-        net.panel_slot(t + 1)
-        if t == 2:
-            net.b_start()
+        net.panel_slot(t + 2)
 
     def forward(lo, dst, rhs):
         for t in range(4):
@@ -460,13 +474,13 @@
                     m[base + i * T : base + (i + 1) * T, i * T :] -= dot(piece[:, lo : lo + T], piece[:, lo:], 0, 0)
                 after(ts)
 
-    net.b_wait()
-    for c, piece in enumerate(spread_rows(bbuf.at[0])):
-        r[:, c * T : (c + 1) * T] = piece
+    for c in range(4):
+        r[:, c * T : (c + 1) * T] = bt[0, c].T
     forward(0, w.at[0:NB], r)
     r[...] = dot(x[...], w[0:NB, :], 0, 0)
-    for c, piece in enumerate(spread_rows(bbuf.at[1])):
-        r[:, c * T : (c + 1) * T] = piece - r[:, c * T : (c + 1) * T]
+    for c in range(4):
+        r[:, c * T : (c + 1) * T] = bt[1, c].T - r[:, c * T : (c + 1) * T]
+    net.panel_slot(10)
     forward(NB, w.at[NB:N2], r)
 
     top_ref[...] = w[pl.ds(pl.multiple_of(jnp.minimum(pr, 1) * NB, NB), NB), :]
@@ -497,7 +511,7 @@
             if t < 3:
                 acc = acc - dot(u[half + a : half + b, b:], q_ref[half + b : half + NB, :])
             q_ref[half + a : half + b, :] = dot(g[half + a : half + b, :], acc, 0, 0)
-    net.panel_slot(9)
+    net.panel_slot(11)
     net.finish()
 
 
@@ -516,8 +530,8 @@
         out_specs=(vmem, vmem, pl.BlockSpec(memory_space=pl.ANY)),
         scratch_shapes=[
             pltpu.VMEM((3, 4, 4, 2, 64, T), f32),
-            pltpu.VMEM((2, 4 * NB, T), f32),
-            pltpu.VMEM((4, T, NB), f32),
+            pltpu.VMEM((4 * NB, T), f32),
+            pltpu.VMEM((2, 4, T, NB), f32),
             pltpu.VMEM((N2, NB), f32),
             pltpu.VMEM((N2, NB), f32),
             pltpu.VMEM((N2, T), f32),
@@ -531,9 +545,10 @@
             dma((3,)),
             dma((3, 13)),
             dma((3, 13)),
-            dma((3,)),
-            dma((2,)),
             dma((4, 2)),
+            dma((2, 4, 2)),
+            dma((2, 4)),
+            dma((4, 3)),
             dma((4,)),
             dma((4, 16)),
             dma((4, 16)),

time: 153 us -> 148 us (0.967)
  Pallas kernels: 153 us -> 147 us
    pallas_call x1, Pallas kernels: 133 us -> 128 us  [factor(): pl.pallas_call(factor_kernel, out_shape=(jax.ShapeDtypeStruct((NB, NB), f...]
where the time goes in v4:
time: 148 us; the launch traced here: 147 us
  Pallas kernels  147 us (99%)
    pallas_call x1, Pallas kernels, factor(): pl.pallas_call(factor_kernel, out_shape=(jax.ShapeDtypeStruct((NB, NB), f...  128 us
    pallas_call x1, Pallas kernels, update(): pl.pallas_call(update_kernel, grid=(8,), out_shape=jax.ShapeDtypeStruct(a...  19.4 us

profile of v4, /device:TPU:7, one launch (start us, length us, event | category | flops | bytes accessed | tf_op | source)
XLA Modules:
  0.0 147.0 jit_solution(13721416192835492999)
XLA Ops:
  0.0 127.6 %shard_map.17 = (f32[512,512]{1,0:T(8,128)S(1)}, f32[1024,512]{1,0:T(8,128)S(1)}, f32[4,4,4,2,64,512]{5,4,3,2,1,0:T(8,128)}) custom-call(f32[16384,128]{1,0:T(8,128)} %bitcast.3), custom_call_target="tpu_custom_call" | custom-call | flops 60000002048 | bytes 10000000 | tf_op jit(solution)/shard_map/pallas_call | solution.py:522
  127.6 19.4 %shard_map.18 = f32[16384,128]{1,0:T(8,128)} custom-call(f32[16384,128]{1,0:T(8,128)} %bitcast.4, f32[8,2,512,512]{3,2,1,0:T(8,128)} %bitcast.5, f32[1024,512]{1,0:T(8,128)S(1)} %get-tuple-element.9.q_ref, f32[512,512]{1,0:T(8,128)S(1)} %get-tuple-element.10.top_ref), custom_call_target="tpu_custom_call" | custom-call | flops 12999999488 | bytes 34000000 | tf_op jit(solution)/shard_map/pallas_call | solution.py:600

commit v5 on v4

--- a/solution.py
+++ b/solution.py
@@ -15,6 +15,15 @@
 
 def dot(a, b, ca=1, cb=0):
     return lax.dot_general(a, b, (((ca,), (cb,)), ((), ())), precision=HI, preferred_element_type=jnp.float32)
+
+
+def dot3(a, b, ca=1, cb=0):
+    (ah, al), (bh, bl) = split(a), split(b)
+
+    def one(p, q):
+        return lax.dot_general(p, q, (((ca,), (cb,)), ((), ())), preferred_element_type=jnp.float32)
+
+    return one(ah, bh) + (one(ah, bl) + one(al, bh))
 
 
 def sub_bcast(x, j):
@@ -336,9 +345,7 @@
         return self.copy(ref, ref, self.c_s.at[s], self.c_r.at[s], self.pr, self.place(self.y, self.z, oc))
 
     def panel_stage(self, s, stage):
-        if stage == 0:
-            self.b_start(s)
-        elif stage == 1:
+        if stage == 1:
             self.b_forward(s)
         elif stage == 2:
             self.b_wait(s)
@@ -358,7 +365,7 @@
 
     def panel_slot(self, slot):
         for s in range(4):
-            if 0 <= slot - s <= 8:
+            if 1 <= slot - s <= 8:
                 self.panel_stage(s, slot - s)
 
     def finish(self):
@@ -401,7 +408,8 @@
     net.barrier()
     net.scatter_start(0)
     net.turn()
-    net.panel_slot(0)
+    for s in range(2):
+        net.b_start(s)
     net.spread_start(0)
     net.scatter_start(1)
     net.scatter_start(2)
@@ -413,39 +421,54 @@
     net.spread_start(2)
     net.gather_wait(0, 1)
     net.gather_start(0, 2)
+    for i in (1, 2):
+        net.spread_wait(i)
+        net.gather_start(i, 0)
     net.panel_slot(1)
+    net.b_start(2)
     net.gather_wait(0, 2)
+    net.panel_slot(2)
+    net.b_start(3)
     for c, piece in enumerate(spread_rows(flat.at[0])):
         m[0:NB, c * T : (c + 1) * T] = piece
 
     def after(t):
         if t == 0:
             for i in (1, 2):
-                net.spread_wait(i)
-                net.gather_start(i, 0)
-        elif t < 3:
+                net.gather_wait(i, 0)
+                net.gather_start(i, 1)
+        elif t == 1:
             for i in (1, 2):
-                net.gather_wait(i, t - 1)
-                net.gather_start(i, t)
-        net.panel_slot(t + 2)
+                net.gather_wait(i, 1)
+                net.gather_start(i, 2)
+        net.panel_slot(t + 3)
 
     def forward(lo, dst, rhs):
         for t in range(4):
             a, b = t * T, (t + 1) * T
             acc = rhs[a:b, :]
             if t:
-                acc = acc - dot(u[lo : lo + a, a:b], dst[0:a, :], 0, 0)
-            dst[a:b, :] = dot(g[lo + a : lo + b, :], acc)
+                acc = acc - dot3(u[lo : lo + a, a:b], dst[0:a, :], 0, 0)
+            dst[a:b, :] = dot3(g[lo + a : lo + b, :], acc)
+
+    row = lax.broadcasted_iota(jnp.int32, (NB, NB), 0)
+    col = lax.broadcasted_iota(jnp.int32, (NB, NB), 1)
+    eye = jnp.where(row == col, 1.0, 0.0)
 
     def solve_second():
         for i in (1, 2):
             net.gather_wait(i, 2)
         for c, piece in enumerate(spread_rows(flat.at[1])):
             r[:, c * T : (c + 1) * T] = piece
+            r[:, NB + c * T : NB + (c + 1) * T] = bt[0, c].T
+        r[:, N2:] = eye
         forward(0, x, r)
-        r[...] = dot(x[...], x[...], 0, 0)
+        r[:, 0:N2] = dot3(x[:, 0:NB], x[:, 0:N2], 0, 0)
         for c, piece in enumerate(spread_rows(flat.at[2])):
-            m[NB:, c * T : (c + 1) * T] = piece - r[:, c * T : (c + 1) * T]
+            at, bat = slice(c * T, (c + 1) * T), slice(NB + c * T, NB + (c + 1) * T)
+            m[NB:, at] = piece - r[:, at]
+            r[:, at] = bt[1, c].T - r[:, bat]
+        r[:, NB:N2] = eye
 
     @pl.loop(0, NT)
     def _(t):
@@ -463,6 +486,8 @@
                 if ts % 4 == 3:
                     if ts == 3:
                         solve_second()
+                    else:
+                        forward(NB, w, r.at[:, 0:N2])
                     after(ts)
                     return
                 base = ts // 4 * NB
@@ -474,16 +499,14 @@
                     m[base + i * T : base + (i + 1) * T, i * T :] -= dot(piece[:, lo : lo + T], piece[:, lo:], 0, 0)
                 after(ts)
 
-    for c in range(4):
-        r[:, c * T : (c + 1) * T] = bt[0, c].T
-    forward(0, w.at[0:NB], r)
-    r[...] = dot(x[...], w[0:NB, :], 0, 0)
-    for c in range(4):
-        r[:, c * T : (c + 1) * T] = bt[1, c].T - r[:, c * T : (c + 1) * T]
-    net.panel_slot(10)
-    forward(NB, w.at[NB:N2], r)
-
-    top_ref[...] = w[pl.ds(pl.multiple_of(jnp.minimum(pr, 1) * NB, NB), NB), :]
+    @pl.when(pr == 0)
+    def _():
+        top_ref[...] = x[:, NB:N2]
+
+    @pl.when(pr > 0)
+    def _():
+        top_ref[...] = w[:, 0:NB]
+
     for k in range(2):
 
         @pl.when((pc == k) & (pr == k))
@@ -498,19 +521,12 @@
 
     @pl.when(pc < 2)
     def _():
-        row = lax.broadcasted_iota(jnp.int32, (N2, NB), 0)
-        col = lax.broadcasted_iota(jnp.int32, (N2, NB), 1)
-        w[...] = jnp.where(row == col + pc * NB, -1.0, 0.0)
-
-    for half in (NB, 0):
-        if half == 0:
-            w[0:NB, :] = w[0:NB, :] - dot(x[...], q_ref[NB:, :])
-        for t in reversed(range(4)):
-            a, b = t * T, (t + 1) * T
-            acc = w[half + a : half + b, :]
-            if t < 3:
-                acc = acc - dot(u[half + a : half + b, b:], q_ref[half + b : half + NB, :])
-            q_ref[half + a : half + b, :] = dot(g[half + a : half + b, :], acc, 0, 0)
+        x[:, NB:N2] = jnp.where(pc == 0, -eye, 0.0)
+        w[:, 0:NB] = jnp.where(pc == 1, -eye, 0.0)
+
+    q_ref[NB:, :] = dot3(w[:, NB:N2], w[:, 0:NB], 0, 0)
+    r[:, 0:NB] = x[:, NB:N2] - dot3(x[:, 0:NB], q_ref[NB:, :])
+    q_ref[0:NB, :] = dot3(x[:, N2:], r[:, 0:NB], 0, 0)
     net.panel_slot(11)
     net.finish()
 
@@ -535,9 +551,9 @@
             pltpu.VMEM((N2, NB), f32),
             pltpu.VMEM((N2, NB), f32),
             pltpu.VMEM((N2, T), f32),
-            pltpu.VMEM((NB, NB), f32),
-            pltpu.VMEM((NB, NB), f32),
-            pltpu.VMEM((N2, NB), f32),
+            pltpu.VMEM((NB, N2 + NB), f32),
+            pltpu.VMEM((NB, N2 + NB), f32),
+            pltpu.VMEM((NB, N2), f32),
             dma((6,)),
             dma((32,)),
             dma((3,)),

time: 148 us -> 136 us (0.919)
  Pallas kernels: 147 us -> 134 us
    pallas_call x1, Pallas kernels: 128 us -> 115 us  [factor(): pl.pallas_call(factor_kernel, out_shape=(jax.ShapeDtypeStruct((NB, NB), f...]
where the time goes in v5:
time: 136 us; the launch traced here: 134 us
  Pallas kernels  134 us (99%)
    pallas_call x1, Pallas kernels, factor(): pl.pallas_call(factor_kernel, out_shape=(jax.ShapeDtypeStruct((NB, NB), f...  115 us
    pallas_call x1, Pallas kernels, update(): pl.pallas_call(update_kernel, grid=(8,), out_shape=jax.ShapeDtypeStruct(a...  19.4 us

profile of v5, /device:TPU:7, one launch (start us, length us, event | category | flops | bytes accessed | tf_op | source)
XLA Modules:
  0.0 134.2 jit_solution(7009394433656590878)
XLA Ops:
  0.0 114.8 %shard_map.17 = (f32[512,512]{1,0:T(8,128)S(1)}, f32[1024,512]{1,0:T(8,128)S(1)}, f32[4,4,4,2,64,512]{5,4,3,2,1,0:T(8,128)}) custom-call(f32[16384,128]{1,0:T(8,128)} %bitcast.3), custom_call_target="tpu_custom_call" | custom-call | flops 60000002048 | bytes 10000000 | tf_op jit(solution)/shard_map/pallas_call | solution.py:538
  114.8 19.4 %shard_map.18 = f32[16384,128]{1,0:T(8,128)} custom-call(f32[16384,128]{1,0:T(8,128)} %bitcast.4, f32[8,2,512,512]{3,2,1,0:T(8,128)} %bitcast.5, f32[1024,512]{1,0:T(8,128)S(1)} %get-tuple-element.9.q_ref, f32[512,512]{1,0:T(8,128)S(1)} %get-tuple-element.10.top_ref), custom_call_target="tpu_custom_call" | custom-call | flops 12999999488 | bytes 34000000 | tf_op jit(solution)/shard_map/pallas_call | solution.py:616

commit v6 on v5

--- a/solution.py
+++ b/solution.py
@@ -8,6 +8,7 @@
 T = 128
 NT = 8
 NB = 512
+HB = 256
 N2 = 1024
 MESH = pl.DeviceIdType.MESH
 ROOTS = ((0, 0), (0, 1), (1, 1))
@@ -603,27 +604,27 @@
         part = mm(ph, h) + (mm(ph, lo) + mm(plo, h))
         acc = part if acc is None else acc + part
     for c in range(4):
-        at = pl.ds(c, NB, stride=4)
+        at = pl.ds(c, HB, stride=4)
         o_ref[at, :] = keep * a_ref[at, :] - acc[:, c * T : (c + 1) * T]
 
-    @pl.when((l == 0) & ((pr == 0) | ((pr == 1) & (pc > 0))))
+    @pl.when((l < 2) & ((pr == 0) | ((pr == 1) & (pc > 0))))
     def _():
         for c in range(4):
-            o_ref[pl.ds(c, NB, stride=4), :] = top_ref[:, c * T : (c + 1) * T]
+            o_ref[pl.ds(c, HB, stride=4), :] = top_ref[:, c * T : (c + 1) * T]
 
 
 def update(a, p, q, top):
     return pl.pallas_call(
         update_kernel,
-        grid=(8,),
+        grid=(16,),
         out_shape=jax.ShapeDtypeStruct(a.shape, jnp.float32),
         in_specs=[
-            pl.BlockSpec((4 * NB, T), lambda l: (l, 0)),
-            pl.BlockSpec((1, 2, NB, NB), lambda l: (l, 0, 0, 0)),
+            pl.BlockSpec((4 * HB, T), lambda l: (l, 0)),
+            pl.BlockSpec((1, 2, HB, NB), lambda l: (l // 2, 0, l % 2, 0)),
             pl.BlockSpec((N2, NB), lambda l: (0, 0)),
-            pl.BlockSpec((NB, NB), lambda l: (0, 0)),
+            pl.BlockSpec((HB, NB), lambda l: (jnp.minimum(l, 1), 0)),
         ],
-        out_specs=pl.BlockSpec((4 * NB, T), lambda l: (l, 0)),
+        out_specs=pl.BlockSpec((4 * HB, T), lambda l: (l, 0)),
         scratch_shapes=[pltpu.VMEM((N2, NB), jnp.bfloat16), pltpu.VMEM((N2, NB), jnp.bfloat16)],
         compiler_params=pltpu.CompilerParams(vmem_limit_bytes=48 << 20),
         cost_estimate=pl.CostEstimate(flops=13_000_000_000, bytes_accessed=34_000_000, transcendentals=0),

time: 136 us -> 141 us (1.037)
  Pallas kernels: 134 us -> 138 us
    pallas_call x1, Pallas kernels: 19.4 us -> 23.3 us  [update(): pl.pallas_call(update_kernel, grid=(16,), out_shape=jax.ShapeDtypeStruct(...]
where the time goes in v6:
time: 141 us; the launch traced here: 138 us
  Pallas kernels  138 us (98%)
    pallas_call x1, Pallas kernels, factor(): pl.pallas_call(factor_kernel, out_shape=(jax.ShapeDtypeStruct((NB, NB), f...  115 us
    pallas_call x1, Pallas kernels, update(): pl.pallas_call(update_kernel, grid=(16,), out_shape=jax.ShapeDtypeStruct(...  23.3 us

profile of v6, /device:TPU:7, one launch (start us, length us, event | category | flops | bytes accessed | tf_op | source)
XLA Modules:
  0.0 138.1 jit_solution(1651283986660691421)
XLA Ops:
  0.0 114.8 %shard_map.17 = (f32[512,512]{1,0:T(8,128)S(1)}, f32[1024,512]{1,0:T(8,128)S(1)}, f32[4,4,4,2,64,512]{5,4,3,2,1,0:T(8,128)}) custom-call(f32[16384,128]{1,0:T(8,128)} %bitcast.3), custom_call_target="tpu_custom_call" | custom-call | flops 60000002048 | bytes 10000000 | tf_op jit(solution)/shard_map/pallas_call | solution.py:539
  114.8 23.3 %shard_map.18 = f32[16384,128]{1,0:T(8,128)} custom-call(f32[16384,128]{1,0:T(8,128)} %bitcast.4, f32[8,2,512,512]{3,2,1,0:T(8,128)} %bitcast.5, f32[1024,512]{1,0:T(8,128)S(1)} %get-tuple-element.9.q_ref, f32[512,512]{1,0:T(8,128)S(1)} %get-tuple-element.10.top_ref), custom_call_target="tpu_custom_call" | custom-call | flops 12999999488 | bytes 34000000 | tf_op jit(solution)/shard_map/pallas_call | solution.py:617
